TPU v7x, 256 devices: a whole 4x4x8 slice. The times are simulated.
256 devices in a mesh: seq: 64 (over z, y, core), mdl: 4 (over x).
Axes of the slice: x: 4, y: 4, z: 8, core: 2. Of those that a mesh axis runs over, the one named last changes fastest.
Arguments:
- tokens: bfloat16 [65536, 4096], P(('seq', 'mdl')), may hold values from -32 to 32
- w_query: bfloat16 [4096, 2048], P('mdl'), may hold values from -0.09375 to 0.09375
- key_weight: bfloat16 [4096, 512], P('mdl'), may hold values from -0.09375 to 0.09375
- value_weight: bfloat16 [4096, 512], P('mdl'), may hold values from -0.09375 to 0.09375
- block_list: int32 [256, 8], P('seq'), may hold values from -1 to 254, as said below
Outputs:
- attended: bfloat16 [65536, 2048], P('seq', 'mdl')
Inputs may be any that keep to these rules, and one draw needn't show every extreme that they name: Row b of block_list, with e = b // 4: its first entry is 0 (the sink block) for b >= 1 and -1 for b = 0; its second is b - 1 for b >= 2 and -1 otherwise; every other entry is -1 or a block j >= 1 with e - 31 <= j // 4 <= e - 2, the named blocks of a row distinct. Over the rows b with b // 4 = e, the blocks j >= 1 named with j // 4 = s number at most one for every s other than e.
All inputs are finite; a program needn't handle non-finite values.
Results may differ from a plain program's by a relative error of at most 0.035.
The roundings to bfloat16 on the way count: a program that leaves them out, or rounds other values in their place, can miss the bound.
Values may be sent and summed in bfloat16 or wider, within the bound.
No kernel may reach another device: no remote copies, remote signals or barrier semaphores. Data moves between devices by JAX's collectives and lax.ppermute only.
A program may use at most 192 MiB of HBM per device.

v0:
```python
import jax
import jax.numpy as jnp
from jax import lax
from jax.sharding import PartitionSpec as P

HEAD_SIZE = 128
BLOCK_TOKENS_SIZE = 256


THETA = 1000000.0


def from_behind(value, axis, steps):
    count = lax.axis_size(axis)
    leading, last = (max(0, -steps), min(count, count - steps))
    return lax.ppermute(value, axis, [(source, source + steps) for source in range(leading, last)])


def spread(block, axis, owner):
    block = jnp.where(lax.axis_index(axis) == owner, block, jnp.zeros_like(block))
    return lax.psum(block, axis)


def apply_rotary(values, token_positions, heads):
    rows = values.shape[0]
    head_dim = values.shape[1] // heads
    half = head_dim // 2
    shaped = values.reshape(rows, heads, head_dim)
    freq = THETA ** (-jnp.arange(half, dtype=jnp.float32) / half)
    angle = token_positions.astype(jnp.float32)[:, None] * freq[None, :]
    cosine = jnp.cos(angle)[:, None, :]
    sine = jnp.sin(angle)[:, None, :]
    first = shaped[..., :half]
    second = shaped[..., half:]
    turned = jnp.concatenate(
        [first * cosine - second * sine, second * cosine + first * sine], axis=-1
    )
    return turned.reshape(rows, heads * head_dim)


def on_device(tokens, w_query, key_weight, value_weight, block_list):
    model_count = lax.axis_size("mdl")
    chain_count = lax.axis_size("seq")
    chain_rank = lax.axis_index("seq")
    tok_rows = tokens.shape[0]
    seq_rows = tok_rows * model_count
    query_heads = w_query.shape[1] // HEAD_SIZE // model_count
    kv_heads = key_weight.shape[1] // HEAD_SIZE // model_count
    block_tokens = lax.all_to_all(tokens, "mdl", split_axis=1, concat_axis=0, tiled=True)
    query_part = jnp.dot(block_tokens, w_query, preferred_element_type=jnp.float32)
    key_part = jnp.dot(block_tokens, key_weight, preferred_element_type=jnp.float32)
    value_part = jnp.dot(block_tokens, value_weight, preferred_element_type=jnp.float32)
    query_full, key_full, value_full = (
        lax.psum_scatter(query_part, "mdl", scatter_dimension=1, tiled=True),
        lax.psum_scatter(key_part, "mdl", scatter_dimension=1, tiled=True),
        lax.psum_scatter(value_part, "mdl", scatter_dimension=1, tiled=True),
    )
    token_positions = chain_rank * seq_rows + jnp.arange(seq_rows, dtype=jnp.int32)
    query_matrix = apply_rotary(query_full, token_positions, query_heads).astype(jnp.bfloat16)
    key = apply_rotary(key_full, token_positions, kv_heads).astype(jnp.bfloat16)
    value_matrix = value_full.astype(jnp.bfloat16)
    span = max(chain_count // 2, 1)
    blocks_here = seq_rows // BLOCK_TOKENS_SIZE
    columns = key.shape[1]
    key_buffer = jnp.zeros((span,) + key.shape, jnp.bfloat16).at[0].set(key)
    value_buffer = jnp.zeros((span,) + value_matrix.shape, jnp.bfloat16).at[0].set(value_matrix)

    def hop(step, carry):
        key_store, value_store, moving_key, moving_value = carry
        moving_key, moving_value = from_behind((moving_key, moving_value), "seq", 1)
        key_store = lax.dynamic_update_index_in_dim(key_store, moving_key, step, 0)
        value_store = lax.dynamic_update_index_in_dim(value_store, moving_value, step, 0)
        return (key_store, value_store, moving_key, moving_value)

    key_buffer, value_buffer, unused_key, unused_value = lax.fori_loop(
        1, span, hop, (key_buffer, value_buffer, key, value_matrix)
    )
    key_flat = key_buffer.reshape(span * blocks_here, BLOCK_TOKENS_SIZE, columns)
    value_flat = value_buffer.reshape(span * blocks_here, BLOCK_TOKENS_SIZE, columns)
    source = chain_rank - block_list // blocks_here
    index = jnp.clip(source * blocks_here + block_list % blocks_here, 0, span * blocks_here - 1)
    sink_key, sink_value = (
        spread(key[:BLOCK_TOKENS_SIZE], "seq", 0),
        spread(value_matrix[:BLOCK_TOKENS_SIZE], "seq", 0),
    )
    head_group = query_heads // kv_heads
    scale = 1.0 / HEAD_SIZE**0.5
    causal = jnp.arange(BLOCK_TOKENS_SIZE)[:, None] >= jnp.arange(BLOCK_TOKENS_SIZE)[None, :]
    own_keys = key.reshape(blocks_here, BLOCK_TOKENS_SIZE, columns)
    own_values = value_matrix.reshape(blocks_here, BLOCK_TOKENS_SIZE, columns)
    blocked_queries = query_matrix.reshape(
        blocks_here, BLOCK_TOKENS_SIZE, kv_heads, head_group, HEAD_SIZE
    )

    def attend(inputs):
        queries, row, row_index, block_key, block_value = inputs
        is_sink = (row == 0)[:, None, None]
        picked_key = jnp.where(is_sink, sink_key[None], jnp.take(key_flat, row_index, axis=0))
        picked_value = jnp.where(is_sink, sink_value[None], jnp.take(value_flat, row_index, axis=0))
        keys = jnp.concatenate([picked_key, block_key[None]], axis=0)
        values = jnp.concatenate([picked_value, block_value[None]], axis=0)
        slots = keys.shape[0]
        keys = keys.reshape(slots, BLOCK_TOKENS_SIZE, kv_heads, HEAD_SIZE)
        values = values.reshape(slots, BLOCK_TOKENS_SIZE, kv_heads, HEAD_SIZE)
        listed = jnp.broadcast_to(
            (row >= 0)[None, :, None], (BLOCK_TOKENS_SIZE, slots - 1, BLOCK_TOKENS_SIZE)
        )
        mask = jnp.concatenate([listed, causal[:, None, :]], axis=1)
        scores = (
            jnp.einsum("tkgd,lukd->kgtlu", queries, keys, preferred_element_type=jnp.float32)
            * scale
        )
        scores = jnp.where(mask[None, None], scores, -jnp.inf)
        top = jnp.max(scores, axis=(-2, -1), keepdims=True)
        weights = jnp.exp(scores - top)
        total = jnp.sum(weights, axis=(-2, -1))
        rounded = weights.astype(jnp.bfloat16)
        summed = jnp.einsum("kgtlu,lukd->tkgd", rounded, values, preferred_element_type=jnp.float32)
        result = summed / jnp.transpose(total, (2, 0, 1))[..., None]
        return result.reshape(BLOCK_TOKENS_SIZE, query_heads * HEAD_SIZE).astype(jnp.bfloat16)

    outputs = lax.map(attend, (blocked_queries, block_list, index, own_keys, own_values))
    return outputs.reshape(seq_rows, query_heads * HEAD_SIZE)


def solution(mesh):
    in_specs = (
        P(("seq", "mdl"), None),
        P("mdl", None),
        P("mdl", None),
        P("mdl", None),
        P("seq", None),
    )
    out_specs = P("seq", "mdl")
    return jax.shard_map(
        on_device, mesh=mesh, in_specs=in_specs, out_specs=out_specs, check_vma=False
    )
```

profile of v0, /device:TPU:128, one launch (start us, length us, event | category | flops | bytes accessed | tf_op | source)
XLA Modules:
  0.0 758.1 jit_solution(6605967872023545763)
XLA Ops:
  6.5 4.2 copy.17
  10.7 30.6 %all_to_all.19 = bf16[256,4,1024]{0,2,1:T(8,128)(2,1)S(1)} all-to-all(bf16[256,4,1024]{0,2,1:T(8,128)(2,1)} %bitcast.135), channel_id=1, replica_groups=mesh['seq'=64,'mdl'=4] {'mdl'}, dimensions={1} | all-to-all | bytes 4194304 | tf_op jit(solution)/shard_map/all_to_all | solution.py:49
  43.8 4.3 fusion.49
  52.2 8.9 %fusion.50 = f32[1024,2048]{1,0:T(8,128)} fusion(bf16[1024,1024]{1,0:T(8,128)(2,1)S(1)} %bitcast.143, bf16[1024,2048]{1,0:T(8,128)(2,1)} %param.16), kind=kOutput, calls=%fused_computation.81 | convolution fusion | flops 4294967296 | bytes 14680064 | tf_op jit(solution)/shard_map/dot_general | solution.py:50
  64.8 15.4 %reduce-scatter.6.cloned.1.call-done = f32[1024,128]{1,0:T(8,128)} async-done(((f32[1024,512]{1,0:T(8,128)}), f32[1024,128]{1,0:T(8,128)}) %reduce-scatter.6.cloned.1.call-update) | async-done | bytes 524304 | tf_op jit(solution)/shard_map/reduce_scatter | solution.py:55
  84.9 30.0 %reduce-scatter.4.cloned.1.call-done = f32[1024,128]{1,0:T(8,128)} async-done(((f32[1024,512]{1,0:T(8,128)}), f32[1024,128]{1,0:T(8,128)}) %reduce-scatter.4.cloned.1.call-update) | async-done | bytes 524304 | tf_op jit(solution)/shard_map/reduce_scatter | solution.py:56
  116.0 5.1 scatter.6
  121.1 5.1 scatter.9
  127.6 72.8 %reduce-scatter.8.cloned.1.call-done = f32[1024,512]{1,0:T(8,128)} async-done(((f32[1024,2048]{1,0:T(8,128)}), f32[1024,512]{1,0:T(8,128)}) %reduce-scatter.8.cloned.1.call-update) | async-done | bytes 2097168 | tf_op jit(solution)/shard_map/reduce_scatter | solution.py:54
  205.7 475.0 %while.32 = (s32[]{:T(128)}, bf16[32,1024,128]{2,1,0:T(8,128)(2,1)}, bf16[32,1024,128]{2,1,0:T(8,128)(2,1)}, bf16[1024,128]{1,0:T(8,128)(2,1)S(1)}, bf16[1024,12...) while((s32[]{:T(128)}, bf16[32,1024,128]{2,1,0:T(8,128)(2,1)}, bf16[32,1024,128]{2,1,0:T(8,128)(2,1)}, ...), condition=%wide.region_5.6_spmd, body=%wide.region_4.0_spmd.sunk | while | flops 5 | bytes 4194519 | solution.py:75
  211.3 5.6 collective-permute-done
  225.1 7.2 collective-permute-done
  240.5 7.2 collective-permute-done
  255.8 7.1 collective-permute-done
  271.1 7.3 collective-permute-done
  286.6 7.2 collective-permute-done
  301.9 7.2 collective-permute-done
  317.3 7.2 collective-permute-done
  332.6 7.2 collective-permute-done
  347.9 7.2 collective-permute-done
  363.4 7.2 collective-permute-done
  378.8 7.1 collective-permute-done
  394.1 7.1 collective-permute-done
  409.4 7.1 collective-permute-done
  424.6 7.1 collective-permute-done
  439.9 7.1 collective-permute-done
  455.2 7.1 collective-permute-done
  470.5 7.1 collective-permute-done
  485.9 7.1 collective-permute-done
  501.1 7.1 collective-permute-done
  516.4 7.1 collective-permute-done
  531.7 7.1 collective-permute-done
  546.9 7.1 collective-permute-done
  562.2 7.1 collective-permute-done
  577.5 7.1 collective-permute-done
  592.8 7.1 collective-permute-done
  608.1 7.1 collective-permute-done
  623.4 7.1 collective-permute-done
  638.6 7.1 collective-permute-done
  653.9 7.1 collective-permute-done
  669.2 7.1 collective-permute-done
  680.7 69.6 %while.33 = (s32[]{:T(128)}, bf16[4,256,512]{2,1,0:T(8,128)(2,1)}, s32[4,8]{1,0:T(4,128)S(1)}, bf16[256,128]{1,0:T(8,128)(2,1)}, s32[4,8]{1,0:T(4,128)S(1)}, /*i...) while((s32[]{:T(128)}, bf16[4,256,512]{2,1,0:T(8,128)(2,1)}, ...), condition=%wide.region_10.12_spmd.clone, body=%wide.region_7.11_spmd.clone.sunk | while | flops 1238236160 | bytes 38167948 | solution.py:122
  680.7 4.0 gather_fusion
  684.7 4.0 gather_fusion.1
  698.1 4.0 gather_fusion
  702.1 4.0 gather_fusion.1
  732.9 4.0 gather_fusion
  737.0 4.0 gather_fusion.1
  (320 shorter events, 322.3 us)
Async XLA Ops:
  6.5 73.7 %reduce-scatter.6.cloned.1.call-start = ((), (), s32[]{:S(2)}) async-start(), calls=%async_computation.5 | async-start | bytes 2621440 | tf_op jit(solution)/shard_map/reduce_scatter | solution.py:55
  48.2 66.7 %reduce-scatter.4.cloned.1.call-start = ((), (), s32[]{:S(2)}) async-start(), calls=%async_computation.4 | async-start | bytes 2621440 | tf_op jit(solution)/shard_map/reduce_scatter | solution.py:56
  52.1 148.2 %reduce-scatter.8.cloned.1.call-start = ((), (), s32[]{:S(2)}) async-start(), calls=%async_computation.6 | async-start | bytes 10485760 | tf_op jit(solution)/shard_map/reduce_scatter | solution.py:54
  61.1 619.6 %all-reduce.5.cloned.1.call-start = ((), (), s32[]{:S(2)}) async-start(), calls=%async_computation.7 | async-start | bytes 262144 | tf_op jit(solution)/shard_map/psum | solution.py:21
  205.7 11.1 %collective-permute-start = (bf16[1024,128]{1,0:T(8,128)(2,1)S(1)}, bf16[1024,128]{1,0:T(8,128)(2,1)S(1)}, u32[]{:S(2)}, u32[]{:S(2)}) collective-permute-start(bf16[1024,128]{1,0:T(8,128)(2,1)S(1)} %get-tuple-element.417), channel_id=1, source_target_pairs={{0,4},{4,8},{8,12},{12,16},{16,20},{20,24},{24,28},{28,32},{32,36}... | collective-permute-start | bytes 786440 | tf_op jit(solution)/shard_map/while/body/eval_jaxpr/ppermute | solution.py:16
  207.8 12.0 %collective-permute-start.1 = (bf16[1024,128]{1,0:T(8,128)(2,1)S(1)}, bf16[1024,128]{1,0:T(8,128)(2,1)S(1)}, u32[]{:S(2)}, u32[]{:S(2)}) collective-permute-start(bf16[1024,128]{1,0:T(8,128)(2,1)S(1)} %get-tuple-element.418), channel_id=1, source_target_pairs={{0,4},{4,8},{8,12},{12,16},{16,20},{20,24},{24,28},{28,32},{32,36}... | collective-permute-start | bytes 786440 | tf_op jit(solution)/shard_map/while/body/eval_jaxpr/ppermute | solution.py:16
  221.2 11.1 %collective-permute-start = (bf16[1024,128]{1,0:T(8,128)(2,1)S(1)}, bf16[1024,128]{1,0:T(8,128)(2,1)S(1)}, u32[]{:S(2)}, u32[]{:S(2)}) collective-permute-start(bf16[1024,128]{1,0:T(8,128)(2,1)S(1)} %get-tuple-element.417), channel_id=1, source_target_pairs={{0,4},{4,8},{8,12},{12,16},{16,20},{20,24},{24,28},{28,32},{32,36}... | collective-permute-start | bytes 786440 | tf_op jit(solution)/shard_map/while/body/eval_jaxpr/ppermute | solution.py:16
  223.2 12.0 %collective-permute-start.1 = (bf16[1024,128]{1,0:T(8,128)(2,1)S(1)}, bf16[1024,128]{1,0:T(8,128)(2,1)S(1)}, u32[]{:S(2)}, u32[]{:S(2)}) collective-permute-start(bf16[1024,128]{1,0:T(8,128)(2,1)S(1)} %get-tuple-element.418), channel_id=1, source_target_pairs={{0,4},{4,8},{8,12},{12,16},{16,20},{20,24},{24,28},{28,32},{32,36}... | collective-permute-start | bytes 786440 | tf_op jit(solution)/shard_map/while/body/eval_jaxpr/ppermute | solution.py:16
  236.6 11.1 %collective-permute-start = (bf16[1024,128]{1,0:T(8,128)(2,1)S(1)}, bf16[1024,128]{1,0:T(8,128)(2,1)S(1)}, u32[]{:S(2)}, u32[]{:S(2)}) collective-permute-start(bf16[1024,128]{1,0:T(8,128)(2,1)S(1)} %get-tuple-element.417), channel_id=1, source_target_pairs={{0,4},{4,8},{8,12},{12,16},{16,20},{20,24},{24,28},{28,32},{32,36}... | collective-permute-start | bytes 786440 | tf_op jit(solution)/shard_map/while/body/eval_jaxpr/ppermute | solution.py:16
  238.5 12.0 %collective-permute-start.1 = (bf16[1024,128]{1,0:T(8,128)(2,1)S(1)}, bf16[1024,128]{1,0:T(8,128)(2,1)S(1)}, u32[]{:S(2)}, u32[]{:S(2)}) collective-permute-start(bf16[1024,128]{1,0:T(8,128)(2,1)S(1)} %get-tuple-element.418), channel_id=1, source_target_pairs={{0,4},{4,8},{8,12},{12,16},{16,20},{20,24},{24,28},{28,32},{32,36}... | collective-permute-start | bytes 786440 | tf_op jit(solution)/shard_map/while/body/eval_jaxpr/ppermute | solution.py:16
  253.9 11.9 %collective-permute-start.1 = (bf16[1024,128]{1,0:T(8,128)(2,1)S(1)}, bf16[1024,128]{1,0:T(8,128)(2,1)S(1)}, u32[]{:S(2)}, u32[]{:S(2)}) collective-permute-start(bf16[1024,128]{1,0:T(8,128)(2,1)S(1)} %get-tuple-element.418), channel_id=1, source_target_pairs={{0,4},{4,8},{8,12},{12,16},{16,20},{20,24},{24,28},{28,32},{32,36}... | collective-permute-start | bytes 786440 | tf_op jit(solution)/shard_map/while/body/eval_jaxpr/ppermute | solution.py:16
  267.3 11.1 %collective-permute-start = (bf16[1024,128]{1,0:T(8,128)(2,1)S(1)}, bf16[1024,128]{1,0:T(8,128)(2,1)S(1)}, u32[]{:S(2)}, u32[]{:S(2)}) collective-permute-start(bf16[1024,128]{1,0:T(8,128)(2,1)S(1)} %get-tuple-element.417), channel_id=1, source_target_pairs={{0,4},{4,8},{8,12},{12,16},{16,20},{20,24},{24,28},{28,32},{32,36}... | collective-permute-start | bytes 786440 | tf_op jit(solution)/shard_map/while/body/eval_jaxpr/ppermute | solution.py:16
  269.2 12.1 %collective-permute-start.1 = (bf16[1024,128]{1,0:T(8,128)(2,1)S(1)}, bf16[1024,128]{1,0:T(8,128)(2,1)S(1)}, u32[]{:S(2)}, u32[]{:S(2)}) collective-permute-start(bf16[1024,128]{1,0:T(8,128)(2,1)S(1)} %get-tuple-element.418), channel_id=1, source_target_pairs={{0,4},{4,8},{8,12},{12,16},{16,20},{20,24},{24,28},{28,32},{32,36}... | collective-permute-start | bytes 786440 | tf_op jit(solution)/shard_map/while/body/eval_jaxpr/ppermute | solution.py:16
  282.7 11.0 %collective-permute-start = (bf16[1024,128]{1,0:T(8,128)(2,1)S(1)}, bf16[1024,128]{1,0:T(8,128)(2,1)S(1)}, u32[]{:S(2)}, u32[]{:S(2)}) collective-permute-start(bf16[1024,128]{1,0:T(8,128)(2,1)S(1)} %get-tuple-element.417), channel_id=1, source_target_pairs={{0,4},{4,8},{8,12},{12,16},{16,20},{20,24},{24,28},{28,32},{32,36}... | collective-permute-start | bytes 786440 | tf_op jit(solution)/shard_map/while/body/eval_jaxpr/ppermute | solution.py:16
  284.7 11.9 %collective-permute-start.1 = (bf16[1024,128]{1,0:T(8,128)(2,1)S(1)}, bf16[1024,128]{1,0:T(8,128)(2,1)S(1)}, u32[]{:S(2)}, u32[]{:S(2)}) collective-permute-start(bf16[1024,128]{1,0:T(8,128)(2,1)S(1)} %get-tuple-element.418), channel_id=1, source_target_pairs={{0,4},{4,8},{8,12},{12,16},{16,20},{20,24},{24,28},{28,32},{32,36}... | collective-permute-start | bytes 786440 | tf_op jit(solution)/shard_map/while/body/eval_jaxpr/ppermute | solution.py:16
  298.1 11.1 %collective-permute-start = (bf16[1024,128]{1,0:T(8,128)(2,1)S(1)}, bf16[1024,128]{1,0:T(8,128)(2,1)S(1)}, u32[]{:S(2)}, u32[]{:S(2)}) collective-permute-start(bf16[1024,128]{1,0:T(8,128)(2,1)S(1)} %get-tuple-element.417), channel_id=1, source_target_pairs={{0,4},{4,8},{8,12},{12,16},{16,20},{20,24},{24,28},{28,32},{32,36}... | collective-permute-start | bytes 786440 | tf_op jit(solution)/shard_map/while/body/eval_jaxpr/ppermute | solution.py:16
  300.0 12.0 %collective-permute-start.1 = (bf16[1024,128]{1,0:T(8,128)(2,1)S(1)}, bf16[1024,128]{1,0:T(8,128)(2,1)S(1)}, u32[]{:S(2)}, u32[]{:S(2)}) collective-permute-start(bf16[1024,128]{1,0:T(8,128)(2,1)S(1)} %get-tuple-element.418), channel_id=1, source_target_pairs={{0,4},{4,8},{8,12},{12,16},{16,20},{20,24},{24,28},{28,32},{32,36}... | collective-permute-start | bytes 786440 | tf_op jit(solution)/shard_map/while/body/eval_jaxpr/ppermute | solution.py:16
  313.4 11.0 %collective-permute-start = (bf16[1024,128]{1,0:T(8,128)(2,1)S(1)}, bf16[1024,128]{1,0:T(8,128)(2,1)S(1)}, u32[]{:S(2)}, u32[]{:S(2)}) collective-permute-start(bf16[1024,128]{1,0:T(8,128)(2,1)S(1)} %get-tuple-element.417), channel_id=1, source_target_pairs={{0,4},{4,8},{8,12},{12,16},{16,20},{20,24},{24,28},{28,32},{32,36}... | collective-permute-start | bytes 786440 | tf_op jit(solution)/shard_map/while/body/eval_jaxpr/ppermute | solution.py:16
  315.3 11.9 %collective-permute-start.1 = (bf16[1024,128]{1,0:T(8,128)(2,1)S(1)}, bf16[1024,128]{1,0:T(8,128)(2,1)S(1)}, u32[]{:S(2)}, u32[]{:S(2)}) collective-permute-start(bf16[1024,128]{1,0:T(8,128)(2,1)S(1)} %get-tuple-element.418), channel_id=1, source_target_pairs={{0,4},{4,8},{8,12},{12,16},{16,20},{20,24},{24,28},{28,32},{32,36}... | collective-permute-start | bytes 786440 | tf_op jit(solution)/shard_map/while/body/eval_jaxpr/ppermute | solution.py:16
  328.7 11.0 %collective-permute-start = (bf16[1024,128]{1,0:T(8,128)(2,1)S(1)}, bf16[1024,128]{1,0:T(8,128)(2,1)S(1)}, u32[]{:S(2)}, u32[]{:S(2)}) collective-permute-start(bf16[1024,128]{1,0:T(8,128)(2,1)S(1)} %get-tuple-element.417), channel_id=1, source_target_pairs={{0,4},{4,8},{8,12},{12,16},{16,20},{20,24},{24,28},{28,32},{32,36}... | collective-permute-start | bytes 786440 | tf_op jit(solution)/shard_map/while/body/eval_jaxpr/ppermute | solution.py:16
  330.6 12.0 %collective-permute-start.1 = (bf16[1024,128]{1,0:T(8,128)(2,1)S(1)}, bf16[1024,128]{1,0:T(8,128)(2,1)S(1)}, u32[]{:S(2)}, u32[]{:S(2)}) collective-permute-start(bf16[1024,128]{1,0:T(8,128)(2,1)S(1)} %get-tuple-element.418), channel_id=1, source_target_pairs={{0,4},{4,8},{8,12},{12,16},{16,20},{20,24},{24,28},{28,32},{32,36}... | collective-permute-start | bytes 786440 | tf_op jit(solution)/shard_map/while/body/eval_jaxpr/ppermute | solution.py:16
  344.1 11.1 %collective-permute-start = (bf16[1024,128]{1,0:T(8,128)(2,1)S(1)}, bf16[1024,128]{1,0:T(8,128)(2,1)S(1)}, u32[]{:S(2)}, u32[]{:S(2)}) collective-permute-start(bf16[1024,128]{1,0:T(8,128)(2,1)S(1)} %get-tuple-element.417), channel_id=1, source_target_pairs={{0,4},{4,8},{8,12},{12,16},{16,20},{20,24},{24,28},{28,32},{32,36}... | collective-permute-start | bytes 786440 | tf_op jit(solution)/shard_map/while/body/eval_jaxpr/ppermute | solution.py:16
  346.0 12.1 %collective-permute-start.1 = (bf16[1024,128]{1,0:T(8,128)(2,1)S(1)}, bf16[1024,128]{1,0:T(8,128)(2,1)S(1)}, u32[]{:S(2)}, u32[]{:S(2)}) collective-permute-start(bf16[1024,128]{1,0:T(8,128)(2,1)S(1)} %get-tuple-element.418), channel_id=1, source_target_pairs={{0,4},{4,8},{8,12},{12,16},{16,20},{20,24},{24,28},{28,32},{32,36}... | collective-permute-start | bytes 786440 | tf_op jit(solution)/shard_map/while/body/eval_jaxpr/ppermute | solution.py:16
  359.6 11.1 %collective-permute-start = (bf16[1024,128]{1,0:T(8,128)(2,1)S(1)}, bf16[1024,128]{1,0:T(8,128)(2,1)S(1)}, u32[]{:S(2)}, u32[]{:S(2)}) collective-permute-start(bf16[1024,128]{1,0:T(8,128)(2,1)S(1)} %get-tuple-element.417), channel_id=1, source_target_pairs={{0,4},{4,8},{8,12},{12,16},{16,20},{20,24},{24,28},{28,32},{32,36}... | collective-permute-start | bytes 786440 | tf_op jit(solution)/shard_map/while/body/eval_jaxpr/ppermute | solution.py:16
  361.5 12.0 %collective-permute-start.1 = (bf16[1024,128]{1,0:T(8,128)(2,1)S(1)}, bf16[1024,128]{1,0:T(8,128)(2,1)S(1)}, u32[]{:S(2)}, u32[]{:S(2)}) collective-permute-start(bf16[1024,128]{1,0:T(8,128)(2,1)S(1)} %get-tuple-element.418), channel_id=1, source_target_pairs={{0,4},{4,8},{8,12},{12,16},{16,20},{20,24},{24,28},{28,32},{32,36}... | collective-permute-start | bytes 786440 | tf_op jit(solution)/shard_map/while/body/eval_jaxpr/ppermute | solution.py:16
  375.0 11.0 %collective-permute-start = (bf16[1024,128]{1,0:T(8,128)(2,1)S(1)}, bf16[1024,128]{1,0:T(8,128)(2,1)S(1)}, u32[]{:S(2)}, u32[]{:S(2)}) collective-permute-start(bf16[1024,128]{1,0:T(8,128)(2,1)S(1)} %get-tuple-element.417), channel_id=1, source_target_pairs={{0,4},{4,8},{8,12},{12,16},{16,20},{20,24},{24,28},{28,32},{32,36}... | collective-permute-start | bytes 786440 | tf_op jit(solution)/shard_map/while/body/eval_jaxpr/ppermute | solution.py:16
  376.9 11.9 %collective-permute-start.1 = (bf16[1024,128]{1,0:T(8,128)(2,1)S(1)}, bf16[1024,128]{1,0:T(8,128)(2,1)S(1)}, u32[]{:S(2)}, u32[]{:S(2)}) collective-permute-start(bf16[1024,128]{1,0:T(8,128)(2,1)S(1)} %get-tuple-element.418), channel_id=1, source_target_pairs={{0,4},{4,8},{8,12},{12,16},{16,20},{20,24},{24,28},{28,32},{32,36}... | collective-permute-start | bytes 786440 | tf_op jit(solution)/shard_map/while/body/eval_jaxpr/ppermute | solution.py:16
  392.2 11.9 %collective-permute-start.1 = (bf16[1024,128]{1,0:T(8,128)(2,1)S(1)}, bf16[1024,128]{1,0:T(8,128)(2,1)S(1)}, u32[]{:S(2)}, u32[]{:S(2)}) collective-permute-start(bf16[1024,128]{1,0:T(8,128)(2,1)S(1)} %get-tuple-element.418), channel_id=1, source_target_pairs={{0,4},{4,8},{8,12},{12,16},{16,20},{20,24},{24,28},{28,32},{32,36}... | collective-permute-start | bytes 786440 | tf_op jit(solution)/shard_map/while/body/eval_jaxpr/ppermute | solution.py:16
  407.4 11.9 %collective-permute-start.1 = (bf16[1024,128]{1,0:T(8,128)(2,1)S(1)}, bf16[1024,128]{1,0:T(8,128)(2,1)S(1)}, u32[]{:S(2)}, u32[]{:S(2)}) collective-permute-start(bf16[1024,128]{1,0:T(8,128)(2,1)S(1)} %get-tuple-element.418), channel_id=1, source_target_pairs={{0,4},{4,8},{8,12},{12,16},{16,20},{20,24},{24,28},{28,32},{32,36}... | collective-permute-start | bytes 786440 | tf_op jit(solution)/shard_map/while/body/eval_jaxpr/ppermute | solution.py:16
  422.7 11.9 %collective-permute-start.1 = (bf16[1024,128]{1,0:T(8,128)(2,1)S(1)}, bf16[1024,128]{1,0:T(8,128)(2,1)S(1)}, u32[]{:S(2)}, u32[]{:S(2)}) collective-permute-start(bf16[1024,128]{1,0:T(8,128)(2,1)S(1)} %get-tuple-element.418), channel_id=1, source_target_pairs={{0,4},{4,8},{8,12},{12,16},{16,20},{20,24},{24,28},{28,32},{32,36}... | collective-permute-start | bytes 786440 | tf_op jit(solution)/shard_map/while/body/eval_jaxpr/ppermute | solution.py:16
  438.0 11.9 %collective-permute-start.1 = (bf16[1024,128]{1,0:T(8,128)(2,1)S(1)}, bf16[1024,128]{1,0:T(8,128)(2,1)S(1)}, u32[]{:S(2)}, u32[]{:S(2)}) collective-permute-start(bf16[1024,128]{1,0:T(8,128)(2,1)S(1)} %get-tuple-element.418), channel_id=1, source_target_pairs={{0,4},{4,8},{8,12},{12,16},{16,20},{20,24},{24,28},{28,32},{32,36}... | collective-permute-start | bytes 786440 | tf_op jit(solution)/shard_map/while/body/eval_jaxpr/ppermute | solution.py:16
  451.4 11.0 %collective-permute-start = (bf16[1024,128]{1,0:T(8,128)(2,1)S(1)}, bf16[1024,128]{1,0:T(8,128)(2,1)S(1)}, u32[]{:S(2)}, u32[]{:S(2)}) collective-permute-start(bf16[1024,128]{1,0:T(8,128)(2,1)S(1)} %get-tuple-element.417), channel_id=1, source_target_pairs={{0,4},{4,8},{8,12},{12,16},{16,20},{20,24},{24,28},{28,32},{32,36}... | collective-permute-start | bytes 786440 | tf_op jit(solution)/shard_map/while/body/eval_jaxpr/ppermute | solution.py:16
  453.3 11.9 %collective-permute-start.1 = (bf16[1024,128]{1,0:T(8,128)(2,1)S(1)}, bf16[1024,128]{1,0:T(8,128)(2,1)S(1)}, u32[]{:S(2)}, u32[]{:S(2)}) collective-permute-start(bf16[1024,128]{1,0:T(8,128)(2,1)S(1)} %get-tuple-element.418), channel_id=1, source_target_pairs={{0,4},{4,8},{8,12},{12,16},{16,20},{20,24},{24,28},{28,32},{32,36}... | collective-permute-start | bytes 786440 | tf_op jit(solution)/shard_map/while/body/eval_jaxpr/ppermute | solution.py:16
  466.7 11.0 %collective-permute-start = (bf16[1024,128]{1,0:T(8,128)(2,1)S(1)}, bf16[1024,128]{1,0:T(8,128)(2,1)S(1)}, u32[]{:S(2)}, u32[]{:S(2)}) collective-permute-start(bf16[1024,128]{1,0:T(8,128)(2,1)S(1)} %get-tuple-element.417), channel_id=1, source_target_pairs={{0,4},{4,8},{8,12},{12,16},{16,20},{20,24},{24,28},{28,32},{32,36}... | collective-permute-start | bytes 786440 | tf_op jit(solution)/shard_map/while/body/eval_jaxpr/ppermute | solution.py:16
  468.6 11.9 %collective-permute-start.1 = (bf16[1024,128]{1,0:T(8,128)(2,1)S(1)}, bf16[1024,128]{1,0:T(8,128)(2,1)S(1)}, u32[]{:S(2)}, u32[]{:S(2)}) collective-permute-start(bf16[1024,128]{1,0:T(8,128)(2,1)S(1)} %get-tuple-element.418), channel_id=1, source_target_pairs={{0,4},{4,8},{8,12},{12,16},{16,20},{20,24},{24,28},{28,32},{32,36}... | collective-permute-start | bytes 786440 | tf_op jit(solution)/shard_map/while/body/eval_jaxpr/ppermute | solution.py:16
  483.9 11.9 %collective-permute-start.1 = (bf16[1024,128]{1,0:T(8,128)(2,1)S(1)}, bf16[1024,128]{1,0:T(8,128)(2,1)S(1)}, u32[]{:S(2)}, u32[]{:S(2)}) collective-permute-start(bf16[1024,128]{1,0:T(8,128)(2,1)S(1)} %get-tuple-element.418), channel_id=1, source_target_pairs={{0,4},{4,8},{8,12},{12,16},{16,20},{20,24},{24,28},{28,32},{32,36}... | collective-permute-start | bytes 786440 | tf_op jit(solution)/shard_map/while/body/eval_jaxpr/ppermute | solution.py:16
  499.2 11.9 %collective-permute-start.1 = (bf16[1024,128]{1,0:T(8,128)(2,1)S(1)}, bf16[1024,128]{1,0:T(8,128)(2,1)S(1)}, u32[]{:S(2)}, u32[]{:S(2)}) collective-permute-start(bf16[1024,128]{1,0:T(8,128)(2,1)S(1)} %get-tuple-element.418), channel_id=1, source_target_pairs={{0,4},{4,8},{8,12},{12,16},{16,20},{20,24},{24,28},{28,32},{32,36}... | collective-permute-start | bytes 786440 | tf_op jit(solution)/shard_map/while/body/eval_jaxpr/ppermute | solution.py:16
  514.5 11.9 %collective-permute-start.1 = (bf16[1024,128]{1,0:T(8,128)(2,1)S(1)}, bf16[1024,128]{1,0:T(8,128)(2,1)S(1)}, u32[]{:S(2)}, u32[]{:S(2)}) collective-permute-start(bf16[1024,128]{1,0:T(8,128)(2,1)S(1)} %get-tuple-element.418), channel_id=1, source_target_pairs={{0,4},{4,8},{8,12},{12,16},{16,20},{20,24},{24,28},{28,32},{32,36}... | collective-permute-start | bytes 786440 | tf_op jit(solution)/shard_map/while/body/eval_jaxpr/ppermute | solution.py:16
  529.7 11.9 %collective-permute-start.1 = (bf16[1024,128]{1,0:T(8,128)(2,1)S(1)}, bf16[1024,128]{1,0:T(8,128)(2,1)S(1)}, u32[]{:S(2)}, u32[]{:S(2)}) collective-permute-start(bf16[1024,128]{1,0:T(8,128)(2,1)S(1)} %get-tuple-element.418), channel_id=1, source_target_pairs={{0,4},{4,8},{8,12},{12,16},{16,20},{20,24},{24,28},{28,32},{32,36}... | collective-permute-start | bytes 786440 | tf_op jit(solution)/shard_map/while/body/eval_jaxpr/ppermute | solution.py:16
  545.0 11.9 %collective-permute-start.1 = (bf16[1024,128]{1,0:T(8,128)(2,1)S(1)}, bf16[1024,128]{1,0:T(8,128)(2,1)S(1)}, u32[]{:S(2)}, u32[]{:S(2)}) collective-permute-start(bf16[1024,128]{1,0:T(8,128)(2,1)S(1)} %get-tuple-element.418), channel_id=1, source_target_pairs={{0,4},{4,8},{8,12},{12,16},{16,20},{20,24},{24,28},{28,32},{32,36}... | collective-permute-start | bytes 786440 | tf_op jit(solution)/shard_map/while/body/eval_jaxpr/ppermute | solution.py:16
  560.3 11.9 %collective-permute-start.1 = (bf16[1024,128]{1,0:T(8,128)(2,1)S(1)}, bf16[1024,128]{1,0:T(8,128)(2,1)S(1)}, u32[]{:S(2)}, u32[]{:S(2)}) collective-permute-start(bf16[1024,128]{1,0:T(8,128)(2,1)S(1)} %get-tuple-element.418), channel_id=1, source_target_pairs={{0,4},{4,8},{8,12},{12,16},{16,20},{20,24},{24,28},{28,32},{32,36}... | collective-permute-start | bytes 786440 | tf_op jit(solution)/shard_map/while/body/eval_jaxpr/ppermute | solution.py:16
  575.6 11.9 %collective-permute-start.1 = (bf16[1024,128]{1,0:T(8,128)(2,1)S(1)}, bf16[1024,128]{1,0:T(8,128)(2,1)S(1)}, u32[]{:S(2)}, u32[]{:S(2)}) collective-permute-start(bf16[1024,128]{1,0:T(8,128)(2,1)S(1)} %get-tuple-element.418), channel_id=1, source_target_pairs={{0,4},{4,8},{8,12},{12,16},{16,20},{20,24},{24,28},{28,32},{32,36}... | collective-permute-start | bytes 786440 | tf_op jit(solution)/shard_map/while/body/eval_jaxpr/ppermute | solution.py:16
  590.9 11.9 %collective-permute-start.1 = (bf16[1024,128]{1,0:T(8,128)(2,1)S(1)}, bf16[1024,128]{1,0:T(8,128)(2,1)S(1)}, u32[]{:S(2)}, u32[]{:S(2)}) collective-permute-start(bf16[1024,128]{1,0:T(8,128)(2,1)S(1)} %get-tuple-element.418), channel_id=1, source_target_pairs={{0,4},{4,8},{8,12},{12,16},{16,20},{20,24},{24,28},{28,32},{32,36}... | collective-permute-start | bytes 786440 | tf_op jit(solution)/shard_map/while/body/eval_jaxpr/ppermute | solution.py:16
  606.2 11.9 %collective-permute-start.1 = (bf16[1024,128]{1,0:T(8,128)(2,1)S(1)}, bf16[1024,128]{1,0:T(8,128)(2,1)S(1)}, u32[]{:S(2)}, u32[]{:S(2)}) collective-permute-start(bf16[1024,128]{1,0:T(8,128)(2,1)S(1)} %get-tuple-element.418), channel_id=1, source_target_pairs={{0,4},{4,8},{8,12},{12,16},{16,20},{20,24},{24,28},{28,32},{32,36}... | collective-permute-start | bytes 786440 | tf_op jit(solution)/shard_map/while/body/eval_jaxpr/ppermute | solution.py:16
  621.5 11.9 %collective-permute-start.1 = (bf16[1024,128]{1,0:T(8,128)(2,1)S(1)}, bf16[1024,128]{1,0:T(8,128)(2,1)S(1)}, u32[]{:S(2)}, u32[]{:S(2)}) collective-permute-start(bf16[1024,128]{1,0:T(8,128)(2,1)S(1)} %get-tuple-element.418), channel_id=1, source_target_pairs={{0,4},{4,8},{8,12},{12,16},{16,20},{20,24},{24,28},{28,32},{32,36}... | collective-permute-start | bytes 786440 | tf_op jit(solution)/shard_map/while/body/eval_jaxpr/ppermute | solution.py:16
  636.7 11.9 %collective-permute-start.1 = (bf16[1024,128]{1,0:T(8,128)(2,1)S(1)}, bf16[1024,128]{1,0:T(8,128)(2,1)S(1)}, u32[]{:S(2)}, u32[]{:S(2)}) collective-permute-start(bf16[1024,128]{1,0:T(8,128)(2,1)S(1)} %get-tuple-element.418), channel_id=1, source_target_pairs={{0,4},{4,8},{8,12},{12,16},{16,20},{20,24},{24,28},{28,32},{32,36}... | collective-permute-start | bytes 786440 | tf_op jit(solution)/shard_map/while/body/eval_jaxpr/ppermute | solution.py:16
  652.0 11.9 %collective-permute-start.1 = (bf16[1024,128]{1,0:T(8,128)(2,1)S(1)}, bf16[1024,128]{1,0:T(8,128)(2,1)S(1)}, u32[]{:S(2)}, u32[]{:S(2)}) collective-permute-start(bf16[1024,128]{1,0:T(8,128)(2,1)S(1)} %get-tuple-element.418), channel_id=1, source_target_pairs={{0,4},{4,8},{8,12},{12,16},{16,20},{20,24},{24,28},{28,32},{32,36}... | collective-permute-start | bytes 786440 | tf_op jit(solution)/shard_map/while/body/eval_jaxpr/ppermute | solution.py:16
  667.3 11.9 %collective-permute-start.1 = (bf16[1024,128]{1,0:T(8,128)(2,1)S(1)}, bf16[1024,128]{1,0:T(8,128)(2,1)S(1)}, u32[]{:S(2)}, u32[]{:S(2)}) collective-permute-start(bf16[1024,128]{1,0:T(8,128)(2,1)S(1)} %get-tuple-element.418), channel_id=1, source_target_pairs={{0,4},{4,8},{8,12},{12,16},{16,20},{20,24},{24,28},{28,32},{32,36}... | collective-permute-start | bytes 786440 | tf_op jit(solution)/shard_map/while/body/eval_jaxpr/ppermute | solution.py:16
  (29 other events, 738.2 us)
Sparse Core Ops, SparseCore 0:
  48.3 31.8 reduce-scatter.5
  82.9 31.9 reduce-scatter.3
  117.5 82.8 reduce-scatter.7
  203.8 169.6 all-reduce.4
where the time goes:
time: 765 us; the launch traced here: 758 us
  waiting for transfers between devices  426 us (56%)
  starting transfers between devices  121 us (16%)
  local copies, waits for them, and re-layouts  104 us (14%)
  matrix products  37.2 us (5%)
  blocking collectives  30.6 us (4%)
  other arithmetic  24.9 us (3%)
  between operations  13.3 us (2%)
    ppermute x62, waiting for transfers between devices, from_behind(): lax.ppermute(value, axis, [(source, source + steps) for source in range(l...  307 us
    ppermute x62, starting transfers between devices, from_behind(): lax.ppermute(value, axis, [(source, source + steps) for source in range(l...  120 us
    reduce_scatter x1, waiting for transfers between devices, on_device(): lax.psum_scatter(query_part, 'mdl', scatter_dimension=1, tiled=True)  72.8 us
    all_to_all x1, blocking collectives, on_device(): lax.all_to_all(tokens, 'mdl', split_axis=1, concat_axis=0, tiled=True)  30.6 us
    reduce_scatter x1, waiting for transfers between devices, on_device(): lax.psum_scatter(value_part, 'mdl', scatter_dimension=1, tiled=True)  30 us
    dynamic_update_slice x31, local copies, waits for them, and re-layouts, hop(): key_store = lax.dynamic_update_index_in_dim(key_store, moving_key, step, 0)  22.6 us
    dynamic_update_slice x31, local copies, waits for them, and re-layouts, hop(): lax.dynamic_update_index_in_dim(value_store, moving_value, step, 0)  22.4 us
    gather x4, local copies, waits for them, and re-layouts, attend(): jnp.take(value_flat, row_index, axis=0)  16.1 us
  transfers between devices with their start and end apart: 66, of which 65 were waited for; matrix products, arithmetic and copies ran while one was open for 11% of the time, Pallas kernels for 0%

commit v1 on v0

v1 whole, which is shorter than its diff:
```python
import functools

import jax
import jax.numpy as jnp
from jax import lax
from jax.experimental import pallas as pl
from jax.experimental.pallas import tpu as pltpu
from jax.sharding import PartitionSpec as P

HEAD_SIZE = 128
BLOCK = 256
THETA = 1000000.0
CORES = 2
YS = 4
ROW = CORES * YS
HOPS = 5
MODELS = 4
FAR = HOPS * YS * CORES
VM = pl.BlockSpec(memory_space=pltpu.VMEM)
SM = pl.BlockSpec(memory_space=pltpu.SMEM)
HBM = pl.BlockSpec(memory_space=pltpu.HBM)
BF = jnp.bfloat16
F32 = jnp.float32


COST = pl.CostEstimate(flops=1, bytes_accessed=1, transcendentals=0)


def params(mib):
    return pltpu.CompilerParams(vmem_limit_bytes=mib * 2**20)


def along_x(value, steps):
    return lax.ppermute(value, "mdl", [(i, (i + steps) % MODELS) for i in range(MODELS)])


def along_z(value, steps):
    count = lax.axis_size("seq")
    return lax.ppermute(value, "seq", [(i, i + ROW * steps) for i in range(count - ROW * steps)])


def along_rows(value, rows, steps):
    pairs = [(i * ROW + j, (i + steps) * ROW + j) for i in rows for j in range(ROW)]
    return lax.ppermute(value, "seq", pairs)


def exchange_y(value):
    count = lax.axis_size("seq")
    groups = [
        [first + y * CORES + c for y in range(YS)] for first in range(0, count, ROW) for c in range(CORES)
    ]
    return lax.all_to_all(value, "seq", split_axis=0, concat_axis=0, axis_index_groups=groups)


def other_core(value):
    count = lax.axis_size("seq")
    return lax.ppermute(value, "seq", [(i, i ^ 1) for i in range(count)])


def columns_of(rank_ref, ahead, width):
    return pl.ds(pl.multiple_of(((rank_ref[0] + ahead) & (MODELS - 1)) * width, width), width)


def split_kernel(aheads, rank_ref, tokens, *refs):
    outs, sems = refs[:-1], refs[-1]
    width = outs[0].shape[1]
    copies = [
        pltpu.make_async_copy(tokens.at[:, columns_of(rank_ref, ahead, width)], outs[i], sems.at[i])
        for i, ahead in enumerate(aheads)
    ]
    for copy in copies:
        copy.start()
    for copy in copies:
        copy.wait()


def split(aheads, rank, tokens):
    shape = jax.ShapeDtypeStruct((tokens.shape[0], tokens.shape[1] // MODELS), BF)
    return pl.pallas_call(
        functools.partial(split_kernel, aheads),
        in_specs=[SM, HBM],
        out_specs=[VM] * len(aheads),
        out_shape=[shape] * len(aheads),
        scratch_shapes=[pltpu.SemaphoreType.DMA((len(aheads),))],
        compiler_params=params(4),
        cost_estimate=COST,
        name="split_columns",
    )(rank, pltpu.with_memory_space_constraint(tokens, pltpu.HBM))


def join_weights_kernel(wk, wv, out):
    for head in range(MODELS):
        column = slice(head * HEAD_SIZE, (head + 1) * HEAD_SIZE)
        out[head, :, :HEAD_SIZE] = wk[:, column]
        out[head, :, HEAD_SIZE:] = wv[:, column]


def join_weights(key_weight, value_weight):
    return pl.pallas_call(
        join_weights_kernel,
        in_specs=[VM] * 2,
        out_specs=VM,
        out_shape=jax.ShapeDtypeStruct((MODELS, key_weight.shape[0], 2 * HEAD_SIZE), BF),
        compiler_params=params(4),
        cost_estimate=COST,
        name="join_weights",
    )(key_weight, value_weight)


def kv_parts_kernel(aheads, rank_ref, t0, t1, t2, t3, w, *outs):
    rank = rank_ref[0]
    rows = t0.shape[0]
    for ahead, out in zip(aheads, outs):
        head = (rank + ahead) & (MODELS - 1)
        for behind, part in enumerate((t0, t1, t2, t3)):
            source = (rank + MODELS - behind) & (MODELS - 1)
            place = pl.ds(pl.multiple_of(source * rows, rows), rows)
            out[place, :] = jnp.dot(part[...], w[head], preferred_element_type=F32).astype(out.dtype)


def kv_parts(aheads, dtype, rank, parts, weights):
    rows = parts[0].shape[0] * MODELS
    shape = jax.ShapeDtypeStruct((rows, 2 * HEAD_SIZE), dtype)
    return pl.pallas_call(
        functools.partial(kv_parts_kernel, aheads),
        in_specs=[SM] + [VM] * 5,
        out_specs=[VM] * len(aheads),
        out_shape=[shape] * len(aheads),
        compiler_params=params(8),
        cost_estimate=COST,
        name="kv_parts",
    )(rank, *parts, weights)


def q_parts_kernel(rank_ref, t0, t1, t2, t3, wq, *outs):
    rank = rank_ref[0]
    rows = t0.shape[0]
    width = outs[0].shape[1]
    for ahead, out in zip((2, 1, 3, 0), outs):
        column = pl.ds(pl.multiple_of(((rank + ahead) & (MODELS - 1)) * width, width), width)
        for behind, part in enumerate((t0, t1, t2, t3)):
            source = (rank + MODELS - behind) & (MODELS - 1)
            place = pl.ds(pl.multiple_of(source * rows, rows), rows)
            out[place, :] = jnp.dot(part[...], wq[:, column], preferred_element_type=F32).astype(BF)


def q_parts(rank, parts, w_query):
    rows = parts[0].shape[0] * MODELS
    return pl.pallas_call(
        q_parts_kernel,
        in_specs=[SM] + [VM] * 5,
        out_specs=[VM] * MODELS,
        out_shape=[jax.ShapeDtypeStruct((rows, w_query.shape[1] // MODELS), BF)] * MODELS,
        compiler_params=params(8),
        cost_estimate=COST,
        name="query_parts",
    )(rank, *parts, w_query)


def turn(u, cosine, sine):
    return u * cosine + pltpu.roll(u, HEAD_SIZE // 2, 1) * sine


def v_join_kernel(a, b, c, own, out):
    out[...] = (own[...] + a[...].astype(F32) + b[...].astype(F32) + c[...].astype(F32)).astype(BF)


def v_join(a, b, c, own):
    return pl.pallas_call(
        v_join_kernel,
        in_specs=[VM] * 4,
        out_specs=VM,
        out_shape=jax.ShapeDtypeStruct(own.shape, BF),
        compiler_params=params(16),
        cost_estimate=COST,
        name="v_join",
    )(a, b, c, own)


def kv_join_kernel(a, b, c, own, cosine, sine, out):
    total = own[...] + a[...].astype(F32) + b[...].astype(F32) + c[...].astype(F32)
    out[:, :HEAD_SIZE] = turn(total[:, :HEAD_SIZE], cosine[...], sine[...]).astype(BF)
    out[:, HEAD_SIZE:] = total[:, HEAD_SIZE:].astype(BF)


def kv_join(a, b, c, own, cosine, sine):
    return pl.pallas_call(
        kv_join_kernel,
        in_specs=[VM] * 6,
        out_specs=VM,
        out_shape=jax.ShapeDtypeStruct(own.shape, BF),
        compiler_params=params(16),
        cost_estimate=COST,
        name="kv_join",
    )(a, b, c, own, cosine, sine)


def q_join_kernel(a, b, c, d, cosine, sine, out):
    for h in range(out.shape[1] // HEAD_SIZE):
        column = slice(h * HEAD_SIZE, (h + 1) * HEAD_SIZE)
        total = a[:, column].astype(F32) + b[:, column].astype(F32) + c[:, column].astype(F32) + d[:, column].astype(F32)
        out[:, column] = turn(total, cosine[...], sine[...]).astype(BF)


def q_join(a, b, c, d, cosine, sine):
    return pl.pallas_call(
        q_join_kernel,
        in_specs=[VM] * 6,
        out_specs=VM,
        out_shape=jax.ShapeDtypeStruct(a.shape, BF),
        compiler_params=params(8),
        cost_estimate=COST,
        name="q_join",
    )(a, b, c, d, cosine, sine)


def select_kernel(hop, pick_ref, held, *refs):
    more, out = refs[:-1], refs[-1]
    for ahead in range(YS):
        for which in range(CORES):
            out[ahead, which] = held[pick_ref[hop, ahead * CORES + which]]
        for i, one in enumerate(more):
            out[ahead, CORES + i] = one[0]


def select_ends_kernel(near_ref, pick_ref, first, last, out):
    for ahead in range(YS):
        for which in range(CORES):
            at = ahead * CORES + which

            @pl.when(near_ref[ahead] == 1)
            def _():
                out[ahead, which] = first[pick_ref[0, at]]

            @pl.when(near_ref[ahead] == 0)
            def _():
                out[ahead, which] = last[pick_ref[HOPS - 1, at]]


def select(body, scalars, held, extra=0, flops=5000000000):
    return pl.pallas_call(
        body,
        in_specs=[SM] * len(scalars) + [VM] * len(held),
        out_specs=VM,
        out_shape=jax.ShapeDtypeStruct((YS, CORES + extra) + held[0].shape[1:], BF),
        compiler_params=params(4),
        cost_estimate=pl.CostEstimate(flops=flops, bytes_accessed=1, transcendentals=0),
        name="select_blocks",
    )(*scalars, *held)


SIDE = (HOPS - 1) * YS
OWN = 2 * SIDE
SINK = OWN + 4
HELD = SINK + 1
LOG2E = 1.4426950408889634
PAIR = 2


def attend_kernel(index_ref, query, own, sink, *refs):
    near, cross = refs[: HOPS - 2], refs[HOPS - 2 : 2 * (HOPS - 2)]
    last_near, last_cross, out, held, sems = refs[2 * (HOPS - 2) :]
    moves = [(own, OWN, 4), (sink, SINK, 1)]
    for side, given in enumerate((near, cross)):
        for i, one in enumerate(given):
            moves += [(one.at[y, pl.ds(side, 1)], side * SIDE + i * YS + y, 1) for y in range(YS)]
    copies = [pltpu.make_async_copy(a, held.at[pl.ds(at, n)], sems.at[i]) for i, (a, at, n) in enumerate(moves)]
    for copy in copies:
        copy.start()
    for side, one in enumerate((last_near, last_cross)):
        for y in range(YS):
            held[side * SIDE + (HOPS - 2) * YS + y] = one[y, side]
    for copy in copies:
        copy.wait()
    slots = 8
    scale = LOG2E / HEAD_SIZE**0.5
    contract = (((1,), (1,)), ((), ()))
    tall = PAIR * BLOCK
    half = BLOCK // 2

    def score(b, first, places, i):
        rows = slice(b * BLOCK, (b + 1) * BLOCK)
        q = jnp.concatenate(
            [query[rows, (first + h) * HEAD_SIZE : (first + h + 1) * HEAD_SIZE] for h in range(PAIR)], axis=0
        )
        at = jnp.maximum(places[i], 0) if i < slots else OWN + b
        s = lax.dot_general(q, held[at, :, :HEAD_SIZE], contract, preferred_element_type=F32)
        if i < slots:
            return s, jnp.where(places[i] >= 0, jnp.maximum(s[:, :half], s[:, half:]), -jnp.inf)
        row = lax.broadcasted_iota(jnp.int32, (tall, BLOCK), 0) & (BLOCK - 1)
        s = jnp.where(row >= lax.broadcasted_iota(jnp.int32, (tall, BLOCK), 1), s, -jnp.inf)
        return s, jnp.maximum(s[:, :half], s[:, half:])

    def scores(work):
        b, first = work
        places = [index_ref[b * slots + i] for i in range(slots)]
        return [functools.partial(score, b, first, places, i) for i in range(slots + 1)], places

    heads = query.shape[1] // HEAD_SIZE
    works = [(b, first) for b in range(query.shape[0] // BLOCK) for first in range(0, heads, PAIR)]
    calls, places = scores(works[0])
    now = [call() for call in calls]
    for n, (b, first) in enumerate(works):
        calls, later = scores(works[n + 1]) if n + 1 < len(works) else ([], None)
        following = []
        top = functools.reduce(jnp.maximum, [m for _, m in now])
        top = jnp.max(top, axis=1, keepdims=True) * scale
        total = jnp.zeros((tall, half), F32)
        summed = jnp.zeros((tall, HEAD_SIZE), F32)
        for i, (s, _) in enumerate(now):
            if calls:
                following.append(calls[i]())
            at = jnp.maximum(places[i], 0) if i < slots else OWN + b
            shift = jnp.where(places[i] >= 0, top, jnp.inf) if i < slots else top
            weight = jnp.exp2(s * scale - shift)
            total = total + (weight[:, :half] + weight[:, half:])
            summed = summed + jnp.dot(weight.astype(BF), held[at, :, HEAD_SIZE:], preferred_element_type=F32)
        result = (summed / jnp.sum(total, axis=1, keepdims=True)).astype(BF)
        for h in range(PAIR):
            column = slice((first + h) * HEAD_SIZE, (first + h + 1) * HEAD_SIZE)
            out[b * BLOCK : (b + 1) * BLOCK, column] = result[h * BLOCK : (h + 1) * BLOCK]
        now, places = following, later


def attend(index, query, own, sink, near, cross):
    early = [pltpu.with_memory_space_constraint(a, pltpu.HBM) for a in (own, sink, *near[:-1], *cross[:-1])]
    return pl.pallas_call(
        attend_kernel,
        in_specs=[SM, VM] + [HBM] * len(early) + [VM] * 2,
        out_specs=VM,
        out_shape=jax.ShapeDtypeStruct(query.shape, BF),
        scratch_shapes=[
            pltpu.VMEM((HELD, BLOCK, 2 * HEAD_SIZE), BF),
            pltpu.SemaphoreType.DMA((2 + 2 * (HOPS - 2) * YS,)),
        ],
        compiler_params=params(40),
        cost_estimate=COST,
        name="attend",
    )(index, query, *early, near[-1], cross[-1])


def tables(first, rows):
    half = HEAD_SIZE // 2
    position = first + jnp.arange(rows, dtype=jnp.int32)
    freq = THETA ** (-jnp.arange(half, dtype=F32) / half)
    angle = position.astype(F32)[:, None] * freq[None, :]
    cosine, sine = jnp.cos(angle), jnp.sin(angle)
    return jnp.concatenate([cosine, cosine], axis=1), jnp.concatenate([-sine, sine], axis=1)


def picks(listed, z):
    source = ROW * (z - jnp.arange(HOPS, dtype=jnp.int32))[:, None] + jnp.arange(ROW, dtype=jnp.int32)[None, :]
    flat = listed.reshape(-1)
    named = (flat[None, None, :] >= 1) & ((flat >> 2)[None, None, :] == source[:, :, None])
    return jnp.max(jnp.where(named, flat & 3, 0), axis=-1)


def on_device(tokens, w_query, key_weight, value_weight, block_list):
    seq = lax.axis_index("seq").astype(jnp.int32)
    rank_ref = lax.axis_index("mdl").astype(jnp.int32).reshape(1)
    rows = tokens.shape[0] * MODELS
    part2, part1, part3 = split((2, 1, 3), rank_ref, tokens)
    part2, part1, part3, seq, block_list = lax.optimization_barrier((part2, part1, part3, seq, block_list))
    part2 = along_x(part2, 2)
    part1 = along_x(part1, 1)
    part3 = along_x(part3, 3)
    [part0] = split((0,), rank_ref, tokens)
    parts = (part0, part1, part2, part3)

    z, y, core = seq >> 3, (seq >> 1) & 3, seq & 1
    mine = picks(block_list, z)
    both = jnp.stack([mine, other_core(mine)])
    wanted = exchange_y(jnp.broadcast_to(both[None], (YS,) + both.shape))
    pick = lax.dynamic_index_in_dim(wanted, y * CORES + core, 3, keepdims=False)
    pick = jnp.transpose(pick, (2, 0, 1)).reshape(HOPS, YS * CORES)
    ahead = jnp.arange(YS, dtype=jnp.int32)
    near_first = ((ahead > y) | ((ahead == y) & (core == 0))).astype(jnp.int32)

    source = block_list >> 2
    hop = z - (source >> 3)
    cross = (source & 1) ^ core
    index = cross * SIDE + jnp.where(hop == 0, HOPS - 2, hop - 1) * YS + ((source >> 1) & 3)
    index = jnp.where(source == seq, OWN + (block_list & 3), index)
    index = jnp.where(block_list == 0, SINK, index)
    index = jnp.where(block_list < 0, -1, index).reshape(-1)

    cosine, sine = tables(seq * rows, rows)
    weights = join_weights(key_weight, value_weight)
    parts, pick, near_first, cosine, sine, index, weights = lax.optimization_barrier(
        (parts, pick, near_first, cosine, sine, index, weights)
    )

    kv2, kv1, kv3 = kv_parts((2, 1, 3), BF, rank_ref, parts, weights)
    parts, kv2 = lax.optimization_barrier((parts, kv2))
    kv2 = along_x(kv2, 2)
    kv1 = along_x(kv1, 1)
    kv3 = along_x(kv3, 3)
    q2, q1, q3, q0 = q_parts(rank_ref, parts, w_query)
    parts, q2 = lax.optimization_barrier((parts, q2))
    [kv0] = kv_parts((0,), F32, rank_ref, parts, weights)
    own = kv_join(kv1, kv2, kv3, kv0, cosine, sine).reshape(4, BLOCK, 2 * HEAD_SIZE)

    own, q2 = lax.optimization_barrier((own, q2))
    q2 = along_x(q2, 2)

    over = lax.ppermute(own[:1], "seq", [(0, 1)])
    held = along_z(own, 1)
    near = []
    for hop in range(1, HOPS - 1):
        onward = along_z(held, 1)
        if hop == 1:
            sent = select(
                functools.partial(select_kernel, hop), [pick], [held, jnp.where(core == 0, own[:1], over)], 1
            )
        else:
            sent = select(
                functools.partial(select_kernel, hop), [pick], [held], flops=10000000000 if hop == 2 else 5000000000
            )
            sent, near[-1] = lax.optimization_barrier((sent, near[-1]))
        if hop == 2:
            sink = near[0][0, CORES:]
            got = along_rows(sink, (0,), 4)
            onward, q2, q1, q3 = lax.optimization_barrier((onward, q2, q1, q3))
            q1 = along_x(q1, 1)
            q3 = along_x(q3, 3)
        if hop == 3:
            sent, got = lax.optimization_barrier((sent, got))
            sink = jnp.where(z == 4, got, sink)
            got = along_rows(sink, (0, 4), 2)
        near.append(exchange_y(sent))
        held = onward
    sent = select(select_ends_kernel, [near_first, pick], [own, held])
    sent, near[-1], got = lax.optimization_barrier((sent, near[-1], got))
    sink = jnp.where((z == 2) | (z == 6), got, sink)
    got = along_rows(sink, (0, 2, 4, 6), 1)
    sink = jnp.where((z & 1) == 1, got, sink)
    near.append(exchange_y(sent))
    query = q_join(q0, q1, q2, q3, cosine, sine)
    near[-1], query, sink = lax.optimization_barrier((near[-1], query, sink))
    across = [other_core(one) for one in near]
    return attend(index, query, own, sink, near, across)


def solution(mesh):
    in_specs = (
        P(("seq", "mdl"), None),
        P("mdl", None),
        P("mdl", None),
        P("mdl", None),
        P("seq", None),
    )
    return jax.shard_map(
        on_device, mesh=mesh, in_specs=in_specs, out_specs=P("seq", "mdl"), check_vma=False
    )
```

time: 765 us -> 187 us (0.24)
  the two profiles are of different devices: /device:TPU:128 before, /device:TPU:1 now
where the time goes in v1:
time: 187 us; the launch traced here: 186 us
  starting transfers between devices  71.2 us (38%)
  waiting for transfers between devices  55.8 us (30%)
  Pallas kernels  43 us (23%)
  local copies, waits for them, and re-layouts  10.3 us (6%)
  other arithmetic  5.03 us (3%)
    ppermute x9, waiting for transfers between devices, along_x(): lax.ppermute(value, 'mdl', [(i, (i + steps) % MODELS) for i in range(MODE...  26.9 us
    all_to_all x5, starting transfers between devices, exchange_y(): lax.all_to_all(value, 'seq', split_axis=0, concat_axis=0, axis_index_grou...  20.7 us
    ppermute x4, starting transfers between devices, along_z(): lax.ppermute(value, 'seq', [(i, i + ROW * steps) for i in range(count - R...  16.8 us
    pallas_call x1, Pallas kernels, attend(): pl.pallas_call(attend_kernel, in_specs=[SM, VM] + [HBM] * len(early) + [V...  16.2 us
    all_to_all x5, waiting for transfers between devices, exchange_y(): lax.all_to_all(value, 'seq', split_axis=0, concat_axis=0, axis_index_grou...  14.2 us
    ppermute x5, starting transfers between devices, other_core(): return lax.ppermute(value, 'seq', [(i, i ^ 1) for i in range(count)])  12.9 us
    ppermute x9, starting transfers between devices, along_x(): lax.ppermute(value, 'mdl', [(i, (i + steps) % MODELS) for i in range(MODE...  10.7 us
    ppermute x3, starting transfers between devices, along_rows(): return lax.ppermute(value, 'seq', pairs)  8.88 us
  transfers between devices with their start and end apart: 27, of which 15 were waited for; matrix products, arithmetic and copies ran while one was open for 4% of the time, Pallas kernels for 11%

profile of v1, /device:TPU:1, one launch (start us, length us, event | category | flops | bytes accessed | tf_op | source)
XLA Modules:
  0.0 185.8 jit_solution(17316181407548148972)
XLA Ops:
  0.0 2.5 %split_columns.3 = (bf16[256,1024]{1,0:T(8,128)(2,1)}, bf16[256,1024]{1,0:T(8,128)(2,1)}, bf16[256,1024]{1,0:T(8,128)(2,1)}) custom-call(s32[1]{0:T(128)} %bitcast.rank_ref, bf16[256,4096]{1,0:T(8,128)(2,1)} %tokens.3), custom_call_target="tpu_custom_call" | custom-call | flops 1 | bytes 1 | tf_op jit(solution)/shard_map/split_columns/pallas_call | solution.py:79
  3.2 3.3 %collective-permute-start.3 = (s32[5,8]{1,0:T(8,128)S(1)}, s32[5,8]{1,0:T(8,128)S(1)}, u32[]{:S(2)}, u32[]{:S(2)}) collective-permute-start(s32[5,8]{1,0:T(8,128)S(1)} %select_reduce_fusion), channel_id=1, source_target_pairs={{0,4},{4,0},{8,12},{12,8},{16,20},{20,16},{24,28},{28,24},{32,36},... | collective-permute-start | bytes 488 | tf_op jit(solution)/shard_map/ppermute | solution.py:57
  6.5 1.9 %collective-permute-start.1 = (bf16[256,1024]{1,0:T(8,128)(2,1)}, bf16[256,1024]{1,0:T(8,128)(2,1)}, u32[]{:S(2)}, u32[]{:S(2)}) collective-permute-start(bf16[256,1024]{1,0:T(8,128)(2,1)} %get-tuple-element.62), channel_id=1, source_target_pairs={{0,2},{1,3},{2,0},{3,1},{4,6},{5,7},{6,4},{7,5},{8,10},{9,11},{10,... | collective-permute-start | bytes 1572872 | tf_op jit(solution)/shard_map/ppermute | solution.py:34
  8.5 1.2 collective-permute-start.2
  9.6 1.9 %fusion = (f32[1024,64]{1,0:T(8,128)S(1)}, f32[1024,64]{1,0:T(8,128)S(1)}, f32[1024,64]{1,0:T(8,128)S(1)}) fusion(f32[64]{0:T(128)S(1)} %multiply_power_fusion, f32[1024]{0:T(1024)S(1)} %add_convert_fusion), kind=kLoop, calls=%fused_computation.4 | loop fusion | flops 131072 | bytes 790784 | tf_op jit(solution)/shard_map/neg | solution.py:348
  13.3 4.2 %all-to-all-start = ((s32[4,2,5,8]{3,1,2,0:T(2,128)}), s32[4,2,5,8]{3,1,2,0:T(2,128)S(1)}, u32[]{:S(2)}, u32[]{:S(2)}) async-start(s32[4,2,5,8]{3,1,2,0:T(2,128)} %broadcast_in_dim.30), calls=%async_computation | async-start | bytes 40960 | tf_op jit(solution)/shard_map/all_to_all | solution.py:52
  18.6 1.2 copy-done.4
  19.8 1.2 copy-done.5
  22.3 10.4 %collective-permute-done.t1 = bf16[256,1024]{1,0:T(8,128)(2,1)} collective-permute-done((bf16[256,1024]{1,0:T(8,128)(2,1)}, bf16[256,1024]{1,0:T(8,128)(2,1)}, u32[]{:S(2)}, u32[]{:S(2)}) %collective-permute-start) | collective-permute-done | bytes 524320 | tf_op jit(solution)/shard_map/ppermute | solution.py:34
  33.1 3.3 %kv_parts.2 = (bf16[1024,256]{1,0:T(8,128)(2,1)S(1)}, bf16[1024,256]{1,0:T(8,128)(2,1)S(1)}, bf16[1024,256]{1,0:T(8,128)(2,1)S(1)}) custom-call(s32[1]{0:T(128)} %bitcast.rank_ref, bf16[256,1024]{1,0:T(8,128)(2,1)S(1)} %split_columns.2.t0, bf16[256,1024]{1,0:T(8,128)(2,1)} %collective-permute-done.t1, bf16[256,1024]{1,0:T(8,128)(2,1)} %collective-permute-done.1.t2, ...), custom_call_target="tpu_custom_call" | custom-call | flops 1 | bytes 1 | tf_op jit(solution)/shard_map/kv_parts/pallas_call | solution.py:124
  37.5 2.6 %collective-permute-start.4 = (bf16[1024,256]{1,0:T(8,128)(2,1)S(1)}, bf16[1024,256]{1,0:T(8,128)(2,1)S(1)}, u32[]{:S(2)}, u32[]{:S(2)}) collective-permute-start(bf16[1024,256]{1,0:T(8,128)(2,1)S(1)} %get-tuple-element.74), channel_id=1, source_target_pairs={{0,1},{1,2},{2,3},{3,0},{4,5},{5,6},{6,7},{7,4},{8,9},{9,10},{10,1... | collective-permute-start | bytes 1572872 | tf_op jit(solution)/shard_map/ppermute | solution.py:34
  40.2 6.0 %query_parts.1 = (bf16[1024,512]{1,0:T(8,128)(2,1)S(1)}, bf16[1024,512]{1,0:T(8,128)(2,1)}, bf16[1024,512]{1,0:T(8,128)(2,1)}, bf16[1024,512]{1,0:T(8,128)(2,1)S(1)}) custom-call(s32[1]{0:T(128)} %bitcast.rank_ref, bf16[256,1024]{1,0:T(8,128)(2,1)S(1)} %split_columns.2.t0, bf16[256,1024]{1,0:T(8,128)(2,1)} %collective-permute-done.t1, ...), custom_call_target="tpu_custom_call" | custom-call | flops 1 | bytes 1 | tf_op jit(solution)/shard_map/query_parts/pallas_call | solution.py:149
  47.1 2.5 %kv_parts.3.own = f32[1024,256]{1,0:T(8,128)S(1)} custom-call(s32[1]{0:T(128)} %bitcast.rank_ref, bf16[256,1024]{1,0:T(8,128)(2,1)S(1)} %split_columns.2.t0, bf16[256,1024]{1,0:T(8,128)(2,1)} %collective-permute-done.t1, bf16[256,1024]{1,0:T(8,128)(2,1)} %collective-permute-done.1.t2, bf16[256,1024]{1,0:T(8,128)(2,1)} %collective-permute-done.2.t3, ...), custom_call_target="tpu_custom_call" | custom-call | flops 1 | bytes 1 | tf_op jit(solution)/shard_map/kv_parts/pallas_call | solution.py:124
  50.2 12.8 %collective-permute-done.4.a = bf16[1024,256]{1,0:T(8,128)(2,1)S(1)} collective-permute-done((bf16[1024,256]{1,0:T(8,128)(2,1)S(1)}, bf16[1024,256]{1,0:T(8,128)(2,1)S(1)}, u32[]{:S(2)}, u32[]{:S(2)}) %collective-permute-start.4) | collective-permute-done | bytes 524320 | tf_op jit(solution)/shard_map/ppermute | solution.py:34
  63.4 3.3 %collective-permute-start.7 = (bf16[4,256,256]{2,1,0:T(8,128)(2,1)S(1)}, bf16[4,256,256]{2,1,0:T(8,128)(2,1)}, u32[]{:S(2)}, u32[]{:S(2)}) collective-permute-start(bf16[4,256,256]{2,1,0:T(8,128)(2,1)S(1)} %bitcast.13), channel_id=1, source_target_pairs={{0,32},{4,36},{8,40},{12,44},{16,48},{20,52},{24,56},{28,60},{32,6... | collective-permute-start | bytes 1572872 | tf_op jit(solution)/shard_map/ppermute | solution.py:39
  66.7 1.3 collective-permute-start.12
  68.1 1.9 %collective-permute-done.12 = bf16[1,256,256]{2,1,0:T(8,128)(2,1)S(1)} collective-permute-done((bf16[1,256,256]{2,1,0:T(8,128)(2,1)S(1)}, bf16[1,256,256]{2,1,0:T(8,128)(2,1)S(1)}, u32[]{:S(2)}, u32[]{:S(2)}) %collective-permute-start.12) | collective-permute-done | bytes 131104 | tf_op jit(solution)/shard_map/ppermute | solution.py:406
  70.0 6.7 %collective-permute-done.7.held = bf16[4,256,256]{2,1,0:T(8,128)(2,1)} collective-permute-done((bf16[4,256,256]{2,1,0:T(8,128)(2,1)S(1)}, bf16[4,256,256]{2,1,0:T(8,128)(2,1)}, u32[]{:S(2)}, u32[]{:S(2)}) %collective-permute-start.7) | collective-permute-done | bytes 524320 | tf_op jit(solution)/shard_map/ppermute | solution.py:39
  76.7 5.0 %collective-permute-start.8 = (bf16[4,256,256]{2,1,0:T(8,128)(2,1)}, bf16[4,256,256]{2,1,0:T(8,128)(2,1)}, u32[]{:S(2)}, u32[]{:S(2)}) collective-permute-start(bf16[4,256,256]{2,1,0:T(8,128)(2,1)} %collective-permute-done.7.held), channel_id=1, source_target_pairs={{0,32},{4,36},{8,40},{12,44},{16,48},{20,52},{24,56},{28,60},{32,6... | collective-permute-start | bytes 1572872 | tf_op jit(solution)/shard_map/ppermute | solution.py:39
  81.7 2.3 %select_blocks.7 = bf16[4,3,256,256]{3,2,1,0:T(8,128)(2,1)} custom-call(s32[5,8]{1,0:T(8,128)S(1)} %copy.19.pick_ref, bf16[4,256,256]{2,1,0:T(8,128)(2,1)} %collective-permute-done.7.held, bf16[1,256,256]{2,1,0:T(8,128)(2,1)S(1)} %broadcast_select_fusion.3.refs_0_), custom_call_target="tpu_custom_call" | custom-call | flops 5000000000 | bytes 1 | tf_op jit(solution)/shard_map/select_blocks/pallas_call | solution.py:241
  84.0 4.5 %all-to-all-start.1 = ((bf16[4,3,256,256]{3,2,1,0:T(8,128)(2,1)}), bf16[4,3,256,256]{3,2,1,0:T(8,128)(2,1)}, u32[]{:S(2)}, u32[]{:S(2)}) async-start(bf16[4,3,256,256]{3,2,1,0:T(8,128)(2,1)} %select_blocks.7), calls=%async_computation.1 | async-start | bytes 3145728 | tf_op jit(solution)/shard_map/all_to_all | solution.py:52
  89.6 1.5 collective-permute-done.8.held
  91.1 4.9 %collective-permute-start.9 = (bf16[4,256,256]{2,1,0:T(8,128)(2,1)}, bf16[4,256,256]{2,1,0:T(8,128)(2,1)}, u32[]{:S(2)}, u32[]{:S(2)}) collective-permute-start(bf16[4,256,256]{2,1,0:T(8,128)(2,1)} %collective-permute-done.8.held), channel_id=1, source_target_pairs={{0,32},{4,36},{8,40},{12,44},{16,48},{20,52},{24,56},{28,60},{32,6... | collective-permute-start | bytes 1572872 | tf_op jit(solution)/shard_map/ppermute | solution.py:39
  96.0 2.1 %select_blocks.6 = bf16[4,2,256,256]{3,2,1,0:T(8,128)(2,1)} custom-call(s32[5,8]{1,0:T(8,128)S(1)} %copy.19.pick_ref, bf16[4,256,256]{2,1,0:T(8,128)(2,1)} %collective-permute-done.8.held), custom_call_target="tpu_custom_call" | custom-call | flops 10000000000 | bytes 1 | tf_op jit(solution)/shard_map/select_blocks/pallas_call | solution.py:241
  98.1 9.4 %all-to-all-done.1.refs_0_ = bf16[4,3,256,256]{3,2,1,0:T(8,128)(2,1)} async-done(((bf16[4,3,256,256]{3,2,1,0:T(8,128)(2,1)}), bf16[4,3,256,256]{3,2,1,0:T(8,128)(2,1)}, u32[]{:S(2)}, u32[]{:S(2)}) %all-to-all-start.1) | async-done | bytes 1572896 | tf_op jit(solution)/shard_map/all_to_all | solution.py:52
  107.5 4.3 %all-to-all-start.2 = ((bf16[4,2,256,256]{3,2,1,0:T(8,128)(2,1)}), bf16[4,2,256,256]{3,2,1,0:T(8,128)(2,1)}, u32[]{:S(2)}, u32[]{:S(2)}) async-start(bf16[4,2,256,256]{3,2,1,0:T(8,128)(2,1)} %select_blocks.6), calls=%async_computation.2 | async-start | bytes 2097152 | tf_op jit(solution)/shard_map/all_to_all | solution.py:52
  111.8 1.3 collective-permute-done.10.c
  113.1 3.5 %collective-permute-start.11 = (bf16[4,256,256]{2,1,0:T(8,128)(2,1)}, bf16[4,256,256]{2,1,0:T(8,128)(2,1)}, u32[]{:S(2)}, u32[]{:S(2)}) collective-permute-start(bf16[4,256,256]{2,1,0:T(8,128)(2,1)} %collective-permute-done.9.held), channel_id=1, source_target_pairs={{0,32},{4,36},{8,40},{12,44},{16,48},{20,52},{24,56},{28,60},{32,6... | collective-permute-start | bytes 1572872 | tf_op jit(solution)/shard_map/ppermute | solution.py:39
  117.6 6.3 %collective-permute-start.13 = (bf16[1,256,256]{2,1,0:T(8,128)(2,1)S(1)}, bf16[1,256,256]{2,1,0:T(8,128)(2,1)S(1)}, u32[]{:S(2)}, u32[]{:S(2)}) collective-permute-start(bf16[1,256,256]{2,1,0:T(8,128)(2,1)S(1)} %slice_bitcast_fusion), channel_id=1, source_target_pairs={{0,128},{4,132},{8,136},{12,140},{16,144},{20,148},{24,152},{28,15... | collective-permute-start | bytes 393224 | tf_op jit(solution)/shard_map/ppermute | solution.py:44
  123.9 2.1 %select_blocks.5 = bf16[4,2,256,256]{3,2,1,0:T(8,128)(2,1)} custom-call(s32[5,8]{1,0:T(8,128)S(1)} %copy.19.pick_ref, bf16[4,256,256]{2,1,0:T(8,128)(2,1)} %collective-permute-done.9.held), custom_call_target="tpu_custom_call" | custom-call | flops 5000000000 | bytes 1 | tf_op jit(solution)/shard_map/select_blocks/pallas_call | solution.py:241
  125.9 1.5 collective-permute-done.13
  127.5 4.3 %all-to-all-start.3 = ((bf16[4,2,256,256]{3,2,1,0:T(8,128)(2,1)}), bf16[4,2,256,256]{3,2,1,0:T(8,128)(2,1)}, u32[]{:S(2)}, u32[]{:S(2)}) async-start(bf16[4,2,256,256]{3,2,1,0:T(8,128)(2,1)} %select_blocks.5), calls=%async_computation.3 | async-start | bytes 2097152 | tf_op jit(solution)/shard_map/all_to_all | solution.py:52
  132.6 1.9 %collective-permute-start.16 = (bf16[1024,512]{1,0:T(8,128)(2,1)}, bf16[1024,512]{1,0:T(8,128)(2,1)}, u32[]{:S(2)}, u32[]{:S(2)}) collective-permute-start(bf16[1024,512]{1,0:T(8,128)(2,1)} %get-tuple-element.104), channel_id=1, source_target_pairs={{0,3},{1,0},{2,1},{3,2},{4,7},{5,4},{6,5},{7,6},{8,11},{9,8},{10,9... | collective-permute-start | bytes 3145736 | tf_op jit(solution)/shard_map/ppermute | solution.py:34
  135.4 1.3 collective-permute-start.14
  136.8 2.2 %select_blocks.4 = bf16[4,2,256,256]{3,2,1,0:T(8,128)(2,1)} custom-call(s32[4]{0:T(128)S(1)} %or_convert_fusion.near_ref, s32[5,8]{1,0:T(8,128)S(1)} %copy.19.pick_ref, bf16[4,256,256]{2,1,0:T(8,128)(2,1)S(1)} %bitcast.16, bf16[4,256,256]{2,1,0:T(8,128)(2,1)} %collective-permute-done.11.last), custom_call_target="tpu_custom_call" | custom-call | flops 5000000000 | bytes 1 | tf_op jit(solution)/shard_map/select_blocks/pallas_call | solution.py:241
  139.0 4.1 %all-to-all-done.3.refs_2_ = bf16[4,2,256,256]{3,2,1,0:T(8,128)(2,1)} async-done(((bf16[4,2,256,256]{3,2,1,0:T(8,128)(2,1)}), bf16[4,2,256,256]{3,2,1,0:T(8,128)(2,1)}, u32[]{:S(2)}, u32[]{:S(2)}) %all-to-all-start.3) | async-done | bytes 1048608 | tf_op jit(solution)/shard_map/all_to_all | solution.py:52
  143.1 3.5 %all-to-all-start.4 = ((bf16[4,2,256,256]{3,2,1,0:T(8,128)(2,1)}), bf16[4,2,256,256]{3,2,1,0:T(8,128)(2,1)S(1)}, u32[]{:S(2)}, u32[]{:S(2)}) async-start(bf16[4,2,256,256]{3,2,1,0:T(8,128)(2,1)} %select_blocks.4), calls=%async_computation.4 | async-start | bytes 2097152 | tf_op jit(solution)/shard_map/all_to_all | solution.py:52
  146.6 4.9 %collective-permute-start.18 = (bf16[4,3,256,256]{3,2,1,0:T(8,128)(2,1)}, bf16[4,3,256,256]{3,2,1,0:T(8,128)(2,1)}, u32[]{:S(2)}, u32[]{:S(2)}) collective-permute-start(bf16[4,3,256,256]{3,2,1,0:T(8,128)(2,1)} %all-to-all-done.1.refs_0_), channel_id=1, source_target_pairs={{0,4},{4,0},{8,12},{12,8},{16,20},{20,16},{24,28},{28,24},{32,36},... | collective-permute-start | bytes 4718600 | tf_op jit(solution)/shard_map/ppermute | solution.py:57
  151.5 1.3 collective-permute-start.17
  152.9 1.4 collective-permute-done.15.b
  155.3 1.2 copy-done.7
  156.6 1.2 copy-done.9
  157.8 1.2 copy-done.11
  159.0 2.0 %q_join.1.query = bf16[1024,512]{1,0:T(8,128)(2,1)S(1)} custom-call(bf16[1024,512]{1,0:T(8,128)(2,1)S(1)} %copy-done.7, bf16[1024,512]{1,0:T(8,128)(2,1)S(1)} %copy-done.11, bf16[1024,512]{1,0:T(8,128)(2,1)S(1)} %copy-done.9, bf16[1024,512]{1,0:T(8,128)(2,1)} %collective-permute-done.16.d, f32[1024,128]{1,0:T(8,128)S(1)} %get-tuple-element.87.cosine, ...), custom_call_target="tpu_custom_call" | custom-call | flops 1 | bytes 1 | tf_op jit(solution)/shard_map/q_join/pallas_call | solution.py:206
  161.1 4.6 %collective-permute-start.20 = (bf16[4,2,256,256]{3,2,1,0:T(8,128)(2,1)}, bf16[4,2,256,256]{3,2,1,0:T(8,128)(2,1)}, u32[]{:S(2)}, u32[]{:S(2)}) collective-permute-start(bf16[4,2,256,256]{3,2,1,0:T(8,128)(2,1)} %all-to-all-done.3.refs_2_), channel_id=1, source_target_pairs={{0,4},{4,0},{8,12},{12,8},{16,20},{20,16},{24,28},{28,24},{32,36},... | collective-permute-start | bytes 3145736 | tf_op jit(solution)/shard_map/ppermute | solution.py:57
  166.3 1.9 %collective-permute-done.20.refs_5_ = bf16[4,2,256,256]{3,2,1,0:T(8,128)(2,1)} collective-permute-done((bf16[4,2,256,256]{3,2,1,0:T(8,128)(2,1)}, bf16[4,2,256,256]{3,2,1,0:T(8,128)(2,1)}, u32[]{:S(2)}, u32[]{:S(2)}) %collective-permute-start.20) | collective-permute-done | bytes 1048608 | tf_op jit(solution)/shard_map/ppermute | solution.py:57
  168.3 1.2 collective-permute-done.21.refs_7_
  169.4 16.2 %attend.1 = bf16[1024,512]{1,0:T(8,128)(2,1)} custom-call(s32[32]{0:T(128)S(1)} %reshape.71.index_ref, bf16[1024,512]{1,0:T(8,128)(2,1)S(1)} %q_join.1.query, bf16[4,256,256]{2,1,0:T(8,128)(2,1)} %bitcast.17, bf16[1,256,256]{2,1,0:T(8,128)(2,1)} %broadcast_select_fusion.1.sink, bf16[4,3,256,256]{3,2,1,0:T(8,128)(2,1)} %all-to-all-done.1.refs_0_, ...), custom_call_target="tpu_custom_call" | custom-call | flops 1 | bytes 1 | tf_op jit(solution)/shard_map/attend/pallas_call | solution.py:327
  (75 shorter events, 13.9 us)
Async XLA Ops:
  0.0 2.6 %copy-start.14 = (s32[4,8]{1,0:T(4,128)S(1)}, s32[4,8]{1,0:T(4,128)}, u32[]{:S(2)}) copy-start(s32[4,8]{1,0:T(4,128)} %param.9) | copy-start | bytes 388
  3.2 9.5 %collective-permute-start.3 = (s32[5,8]{1,0:T(8,128)S(1)}, s32[5,8]{1,0:T(8,128)S(1)}, u32[]{:S(2)}, u32[]{:S(2)}) collective-permute-start(s32[5,8]{1,0:T(8,128)S(1)} %select_reduce_fusion), channel_id=1, source_target_pairs={{0,4},{4,0},{8,12},{12,8},{16,20},{20,16},{24,28},{28,24},{32,36},... | collective-permute-start | bytes 488 | tf_op jit(solution)/shard_map/ppermute | solution.py:57
  6.5 26.2 %collective-permute-start = (bf16[256,1024]{1,0:T(8,128)(2,1)}, bf16[256,1024]{1,0:T(8,128)(2,1)}, u32[]{:S(2)}, u32[]{:S(2)}) collective-permute-start(bf16[256,1024]{1,0:T(8,128)(2,1)} %get-tuple-element.61), channel_id=1, source_target_pairs={{0,1},{1,2},{2,3},{3,0},{4,5},{5,6},{6,7},{7,4},{8,9},{9,10},{10,1... | collective-permute-start | bytes 1572872 | tf_op jit(solution)/shard_map/ppermute | solution.py:34
  6.5 26.2 %collective-permute-start.1 = (bf16[256,1024]{1,0:T(8,128)(2,1)}, bf16[256,1024]{1,0:T(8,128)(2,1)}, u32[]{:S(2)}, u32[]{:S(2)}) collective-permute-start(bf16[256,1024]{1,0:T(8,128)(2,1)} %get-tuple-element.62), channel_id=1, source_target_pairs={{0,2},{1,3},{2,0},{3,1},{4,6},{5,7},{6,4},{7,5},{8,10},{9,11},{10,... | collective-permute-start | bytes 1572872 | tf_op jit(solution)/shard_map/ppermute | solution.py:34
  8.5 24.6 %collective-permute-start.2 = (bf16[256,1024]{1,0:T(8,128)(2,1)}, bf16[256,1024]{1,0:T(8,128)(2,1)}, u32[]{:S(2)}, u32[]{:S(2)}) collective-permute-start(bf16[256,1024]{1,0:T(8,128)(2,1)} %get-tuple-element.63), channel_id=1, source_target_pairs={{0,3},{1,0},{2,1},{3,2},{4,7},{5,4},{6,5},{7,6},{8,11},{9,8},{10,9... | collective-permute-start | bytes 1572872 | tf_op jit(solution)/shard_map/ppermute | solution.py:34
  13.3 8.8 %all-to-all-start = ((s32[4,2,5,8]{3,1,2,0:T(2,128)}), s32[4,2,5,8]{3,1,2,0:T(2,128)S(1)}, u32[]{:S(2)}, u32[]{:S(2)}) async-start(s32[4,2,5,8]{3,1,2,0:T(2,128)} %broadcast_in_dim.30), calls=%async_computation | async-start | bytes 40960 | tf_op jit(solution)/shard_map/all_to_all | solution.py:52
  18.6 1.2 copy-start.4
  19.8 1.2 copy-start.5
  33.1 7.1 %copy-start.2 = (bf16[1024,2048]{1,0:T(8,128)(2,1)S(1)}, bf16[1024,2048]{1,0:T(8,128)(2,1)}, u32[]{:S(2)}) copy-start(bf16[1024,2048]{1,0:T(8,128)(2,1)} %wq.1) | copy-start | bytes 12582916
  36.4 13.9 %collective-permute-start.5 = (bf16[1024,256]{1,0:T(8,128)(2,1)S(1)}, bf16[1024,256]{1,0:T(8,128)(2,1)S(1)}, u32[]{:S(2)}, u32[]{:S(2)}) collective-permute-start(bf16[1024,256]{1,0:T(8,128)(2,1)S(1)} %get-tuple-element.76), channel_id=1, source_target_pairs={{0,2},{1,3},{2,0},{3,1},{4,6},{5,7},{6,4},{7,5},{8,10},{9,11},{10,... | collective-permute-start | bytes 1572872 | tf_op jit(solution)/shard_map/ppermute | solution.py:34
  37.5 25.6 %collective-permute-start.4 = (bf16[1024,256]{1,0:T(8,128)(2,1)S(1)}, bf16[1024,256]{1,0:T(8,128)(2,1)S(1)}, u32[]{:S(2)}, u32[]{:S(2)}) collective-permute-start(bf16[1024,256]{1,0:T(8,128)(2,1)S(1)} %get-tuple-element.74), channel_id=1, source_target_pairs={{0,1},{1,2},{2,3},{3,0},{4,5},{5,6},{6,7},{7,4},{8,9},{9,10},{10,1... | collective-permute-start | bytes 1572872 | tf_op jit(solution)/shard_map/ppermute | solution.py:34
  40.1 23.0 %collective-permute-start.6 = (bf16[1024,256]{1,0:T(8,128)(2,1)S(1)}, bf16[1024,256]{1,0:T(8,128)(2,1)S(1)}, u32[]{:S(2)}, u32[]{:S(2)}) collective-permute-start(bf16[1024,256]{1,0:T(8,128)(2,1)S(1)} %get-tuple-element.77), channel_id=1, source_target_pairs={{0,3},{1,0},{2,1},{3,2},{4,7},{5,4},{6,5},{7,6},{8,11},{9,8},{10,9... | collective-permute-start | bytes 1572872 | tf_op jit(solution)/shard_map/ppermute | solution.py:34
  46.1 1.0 copy-start.6
  47.1 2.5 %copy-start.12 = (bf16[1024,512]{1,0:T(8,128)(2,1)}, bf16[1024,512]{1,0:T(8,128)(2,1)S(1)}, u32[]{:S(2)}) copy-start(bf16[1024,512]{1,0:T(8,128)(2,1)S(1)} %get-tuple-element.91) | copy-start | bytes 3145732
  47.1 15.9 %copy-start = (f32[1024,128]{1,0:T(8,128)S(1)}, f32[1024,128]{1,0:T(8,128)}, u32[]{:S(2)}) copy-start(f32[1024,128]{1,0:T(8,128)} %get-tuple-element.88.sine) | copy-start | bytes 1572868
  63.4 73.3 %copy-start.3 = (bf16[1024,256]{1,0:T(8,128)(2,1)}, bf16[1024,256]{1,0:T(8,128)(2,1)S(1)}, u32[]{:S(2)}) copy-start(bf16[1024,256]{1,0:T(8,128)(2,1)S(1)} %kv_join.1) | copy-start | bytes 1572868
  63.4 13.3 %collective-permute-start.7 = (bf16[4,256,256]{2,1,0:T(8,128)(2,1)S(1)}, bf16[4,256,256]{2,1,0:T(8,128)(2,1)}, u32[]{:S(2)}, u32[]{:S(2)}) collective-permute-start(bf16[4,256,256]{2,1,0:T(8,128)(2,1)S(1)} %bitcast.13), channel_id=1, source_target_pairs={{0,32},{4,36},{8,40},{12,44},{16,48},{20,52},{24,56},{28,60},{32,6... | collective-permute-start | bytes 1572872 | tf_op jit(solution)/shard_map/ppermute | solution.py:39
  66.7 3.2 %collective-permute-start.12 = (bf16[1,256,256]{2,1,0:T(8,128)(2,1)S(1)}, bf16[1,256,256]{2,1,0:T(8,128)(2,1)S(1)}, u32[]{:S(2)}, u32[]{:S(2)}) collective-permute-start(bf16[1,256,256]{2,1,0:T(8,128)(2,1)S(1)} %slice.7), channel_id=1, source_target_pairs={{0,4},{1,5},{2,6},{3,7}} | collective-permute-start | bytes 393224 | tf_op jit(solution)/shard_map/ppermute | solution.py:406
  76.7 14.4 %collective-permute-start.8 = (bf16[4,256,256]{2,1,0:T(8,128)(2,1)}, bf16[4,256,256]{2,1,0:T(8,128)(2,1)}, u32[]{:S(2)}, u32[]{:S(2)}) collective-permute-start(bf16[4,256,256]{2,1,0:T(8,128)(2,1)} %collective-permute-done.7.held), channel_id=1, source_target_pairs={{0,32},{4,36},{8,40},{12,44},{16,48},{20,52},{24,56},{28,60},{32,6... | collective-permute-start | bytes 1572872 | tf_op jit(solution)/shard_map/ppermute | solution.py:39
  84.0 4.5 %copy-start.13 = (bf16[1024,512]{1,0:T(8,128)(2,1)S(1)}, bf16[1024,512]{1,0:T(8,128)(2,1)}, u32[]{:S(2)}) copy-start(bf16[1024,512]{1,0:T(8,128)(2,1)} %copy-done.12) | copy-start | bytes 3145732
  84.0 23.5 %all-to-all-start.1 = ((bf16[4,3,256,256]{3,2,1,0:T(8,128)(2,1)}), bf16[4,3,256,256]{3,2,1,0:T(8,128)(2,1)}, u32[]{:S(2)}, u32[]{:S(2)}) async-start(bf16[4,3,256,256]{3,2,1,0:T(8,128)(2,1)} %select_blocks.7), calls=%async_computation.1 | async-start | bytes 3145728 | tf_op jit(solution)/shard_map/all_to_all | solution.py:52
  88.5 24.6 %collective-permute-start.10 = (bf16[1024,512]{1,0:T(8,128)(2,1)S(1)}, bf16[1024,512]{1,0:T(8,128)(2,1)S(1)}, u32[]{:S(2)}, u32[]{:S(2)}) collective-permute-start(bf16[1024,512]{1,0:T(8,128)(2,1)S(1)} %copy-done.13), channel_id=1, source_target_pairs={{0,2},{1,3},{2,0},{3,1},{4,6},{5,7},{6,4},{7,5},{8,10},{9,11},{10,... | collective-permute-start | bytes 3145736 | tf_op jit(solution)/shard_map/ppermute | solution.py:34
  91.1 22.0 %collective-permute-start.9 = (bf16[4,256,256]{2,1,0:T(8,128)(2,1)}, bf16[4,256,256]{2,1,0:T(8,128)(2,1)}, u32[]{:S(2)}, u32[]{:S(2)}) collective-permute-start(bf16[4,256,256]{2,1,0:T(8,128)(2,1)} %collective-permute-done.8.held), channel_id=1, source_target_pairs={{0,32},{4,36},{8,40},{12,44},{16,48},{20,52},{24,56},{28,60},{32,6... | collective-permute-start | bytes 1572872 | tf_op jit(solution)/shard_map/ppermute | solution.py:39
  107.5 18.4 %all-to-all-start.2 = ((bf16[4,2,256,256]{3,2,1,0:T(8,128)(2,1)}), bf16[4,2,256,256]{3,2,1,0:T(8,128)(2,1)}, u32[]{:S(2)}, u32[]{:S(2)}) async-start(bf16[4,2,256,256]{3,2,1,0:T(8,128)(2,1)} %select_blocks.6), calls=%async_computation.2 | async-start | bytes 2097152 | tf_op jit(solution)/shard_map/all_to_all | solution.py:52
  113.1 12.9 %copy-start.8 = (bf16[1024,512]{1,0:T(8,128)(2,1)}, bf16[1024,512]{1,0:T(8,128)(2,1)S(1)}, u32[]{:S(2)}) copy-start(bf16[1024,512]{1,0:T(8,128)(2,1)S(1)} %collective-permute-done.10.c) | copy-start | bytes 3145732
  113.1 23.6 %collective-permute-start.11 = (bf16[4,256,256]{2,1,0:T(8,128)(2,1)}, bf16[4,256,256]{2,1,0:T(8,128)(2,1)}, u32[]{:S(2)}, u32[]{:S(2)}) collective-permute-start(bf16[4,256,256]{2,1,0:T(8,128)(2,1)} %collective-permute-done.9.held), channel_id=1, source_target_pairs={{0,32},{4,36},{8,40},{12,44},{16,48},{20,52},{24,56},{28,60},{32,6... | collective-permute-start | bytes 1572872 | tf_op jit(solution)/shard_map/ppermute | solution.py:39
  117.6 9.9 %collective-permute-start.13 = (bf16[1,256,256]{2,1,0:T(8,128)(2,1)S(1)}, bf16[1,256,256]{2,1,0:T(8,128)(2,1)S(1)}, u32[]{:S(2)}, u32[]{:S(2)}) collective-permute-start(bf16[1,256,256]{2,1,0:T(8,128)(2,1)S(1)} %slice_bitcast_fusion), channel_id=1, source_target_pairs={{0,128},{4,132},{8,136},{12,140},{16,144},{20,148},{24,152},{28,15... | collective-permute-start | bytes 393224 | tf_op jit(solution)/shard_map/ppermute | solution.py:44
  127.5 15.6 %all-to-all-start.3 = ((bf16[4,2,256,256]{3,2,1,0:T(8,128)(2,1)}), bf16[4,2,256,256]{3,2,1,0:T(8,128)(2,1)}, u32[]{:S(2)}, u32[]{:S(2)}) async-start(bf16[4,2,256,256]{3,2,1,0:T(8,128)(2,1)} %select_blocks.5), calls=%async_computation.3 | async-start | bytes 2097152 | tf_op jit(solution)/shard_map/all_to_all | solution.py:52
  131.8 22.6 %collective-permute-start.15 = (bf16[1024,512]{1,0:T(8,128)(2,1)}, bf16[1024,512]{1,0:T(8,128)(2,1)S(1)}, u32[]{:S(2)}, u32[]{:S(2)}) collective-permute-start(bf16[1024,512]{1,0:T(8,128)(2,1)} %get-tuple-element.102), channel_id=1, source_target_pairs={{0,1},{1,2},{2,3},{3,0},{4,5},{5,6},{6,7},{7,4},{8,9},{9,10},{10,1... | collective-permute-start | bytes 3145736 | tf_op jit(solution)/shard_map/ppermute | solution.py:34
  132.6 22.7 %collective-permute-start.16 = (bf16[1024,512]{1,0:T(8,128)(2,1)}, bf16[1024,512]{1,0:T(8,128)(2,1)}, u32[]{:S(2)}, u32[]{:S(2)}) collective-permute-start(bf16[1024,512]{1,0:T(8,128)(2,1)} %get-tuple-element.104), channel_id=1, source_target_pairs={{0,3},{1,0},{2,1},{3,2},{4,7},{5,4},{6,5},{7,6},{8,11},{9,8},{10,9... | collective-permute-start | bytes 3145736 | tf_op jit(solution)/shard_map/ppermute | solution.py:34
  135.4 3.6 %collective-permute-start.14 = (bf16[1,256,256]{2,1,0:T(8,128)(2,1)S(1)}, bf16[1,256,256]{2,1,0:T(8,128)(2,1)S(1)}, u32[]{:S(2)}, u32[]{:S(2)}) collective-permute-start(bf16[1,256,256]{2,1,0:T(8,128)(2,1)S(1)} %broadcast_select_fusion.2), channel_id=1, source_target_pairs={{0,64},{4,68},{8,72},{12,76},{16,80},{20,84},{24,88},{28,92},{128,... | collective-permute-start | bytes 393224 | tf_op jit(solution)/shard_map/ppermute | solution.py:44
  139.0 16.3 %copy-start.1 = (f32[1024,128]{1,0:T(8,128)S(1)}, f32[1024,128]{1,0:T(8,128)}, u32[]{:S(2)}) copy-start(f32[1024,128]{1,0:T(8,128)} %get-tuple-element.88.sine) | copy-start | bytes 1572868
  143.1 23.2 %all-to-all-start.4 = ((bf16[4,2,256,256]{3,2,1,0:T(8,128)(2,1)}), bf16[4,2,256,256]{3,2,1,0:T(8,128)(2,1)S(1)}, u32[]{:S(2)}, u32[]{:S(2)}) async-start(bf16[4,2,256,256]{3,2,1,0:T(8,128)(2,1)} %select_blocks.4), calls=%async_computation.4 | async-start | bytes 2097152 | tf_op jit(solution)/shard_map/all_to_all | solution.py:52
  146.6 19.7 %collective-permute-start.18 = (bf16[4,3,256,256]{3,2,1,0:T(8,128)(2,1)}, bf16[4,3,256,256]{3,2,1,0:T(8,128)(2,1)}, u32[]{:S(2)}, u32[]{:S(2)}) collective-permute-start(bf16[4,3,256,256]{3,2,1,0:T(8,128)(2,1)} %all-to-all-done.1.refs_0_), channel_id=1, source_target_pairs={{0,4},{4,0},{8,12},{12,8},{16,20},{20,16},{24,28},{28,24},{32,36},... | collective-permute-start | bytes 4718600 | tf_op jit(solution)/shard_map/ppermute | solution.py:57
  151.5 14.1 %collective-permute-start.17 = (bf16[1,256,256]{2,1,0:T(8,128)(2,1)S(1)}, bf16[1,256,256]{2,1,0:T(8,128)(2,1)S(1)}, u32[]{:S(2)}, u32[]{:S(2)}) collective-permute-start(bf16[1,256,256]{2,1,0:T(8,128)(2,1)S(1)} %broadcast_select_fusion), channel_id=1, source_target_pairs={{0,32},{4,36},{8,40},{12,44},{16,48},{20,52},{24,56},{28,60},{64,9... | collective-permute-start | bytes 393224 | tf_op jit(solution)/shard_map/ppermute | solution.py:44
  152.8 13.5 %collective-permute-start.19 = (bf16[4,2,256,256]{3,2,1,0:T(8,128)(2,1)}, bf16[4,2,256,256]{3,2,1,0:T(8,128)(2,1)}, u32[]{:S(2)}, u32[]{:S(2)}) collective-permute-start(bf16[4,2,256,256]{3,2,1,0:T(8,128)(2,1)} %all-to-all-done.2.refs_1_), channel_id=1, source_target_pairs={{0,4},{4,0},{8,12},{12,8},{16,20},{20,16},{24,28},{28,24},{32,36},... | collective-permute-start | bytes 3145736 | tf_op jit(solution)/shard_map/ppermute | solution.py:57
  154.4 1.0 copy-start.10
  155.3 1.2 copy-start.7
  156.6 1.2 copy-start.9
  157.8 1.2 copy-start.11
  161.1 7.2 %collective-permute-start.20 = (bf16[4,2,256,256]{3,2,1,0:T(8,128)(2,1)}, bf16[4,2,256,256]{3,2,1,0:T(8,128)(2,1)}, u32[]{:S(2)}, u32[]{:S(2)}) collective-permute-start(bf16[4,2,256,256]{3,2,1,0:T(8,128)(2,1)} %all-to-all-done.3.refs_2_), channel_id=1, source_target_pairs={{0,4},{4,0},{8,12},{12,8},{16,20},{20,16},{24,28},{28,24},{32,36},... | collective-permute-start | bytes 3145736 | tf_op jit(solution)/shard_map/ppermute | solution.py:57
  166.3 3.1 %collective-permute-start.21 = (bf16[4,2,256,256]{3,2,1,0:T(8,128)(2,1)S(1)}, bf16[4,2,256,256]{3,2,1,0:T(8,128)(2,1)S(1)}, u32[]{:S(2)}, u32[]{:S(2)}) collective-permute-start(bf16[4,2,256,256]{3,2,1,0:T(8,128)(2,1)S(1)} %all-to-all-done.4.refs_6_), channel_id=1, source_target_pairs={{0,4},{4,0},{8,12},{12,8},{16,20},{20,16},{24,28},{28,24},{32,36},... | collective-permute-start | bytes 3145736 | tf_op jit(solution)/shard_map/ppermute | solution.py:57

commit v2 on v1

--- a/solution.py
+++ b/solution.py
@@ -214,13 +214,10 @@
     )(a, b, c, d, cosine, sine)
 
 
-def select_kernel(hop, pick_ref, held, *refs):
-    more, out = refs[:-1], refs[-1]
+def select_kernel(hop, pick_ref, held, out):
     for ahead in range(YS):
         for which in range(CORES):
             out[ahead, which] = held[pick_ref[hop, ahead * CORES + which]]
-        for i, one in enumerate(more):
-            out[ahead, CORES + i] = one[0]
 
 
 def select_ends_kernel(near_ref, pick_ref, first, last, out):
@@ -237,12 +234,12 @@
                 out[ahead, which] = last[pick_ref[HOPS - 1, at]]
 
 
-def select(body, scalars, held, extra=0, flops=5000000000):
+def select(body, scalars, held, flops=5000000000):
     return pl.pallas_call(
         body,
         in_specs=[SM] * len(scalars) + [VM] * len(held),
         out_specs=VM,
-        out_shape=jax.ShapeDtypeStruct((YS, CORES + extra) + held[0].shape[1:], BF),
+        out_shape=jax.ShapeDtypeStruct((YS, CORES) + held[0].shape[1:], BF),
         compiler_params=params(4),
         cost_estimate=pl.CostEstimate(flops=flops, bytes_accessed=1, transcendentals=0),
         name="select_blocks",
@@ -403,22 +400,21 @@
     own, q2 = lax.optimization_barrier((own, q2))
     q2 = along_x(q2, 2)
 
-    over = lax.ppermute(own[:1], "seq", [(0, 1)])
     held = along_z(own, 1)
+    sink = jnp.where(core == 0, own[:1], lax.ppermute(own[:1], "seq", [(0, 1)]))
+    along_y = [lax.ppermute(sink, "seq", [(c, to * CORES + c) for c in range(CORES)]) for to in range(1, YS)]
     near = []
     for hop in range(1, HOPS - 1):
         onward = along_z(held, 1)
-        if hop == 1:
-            sent = select(
-                functools.partial(select_kernel, hop), [pick], [held, jnp.where(core == 0, own[:1], over)], 1
-            )
-        else:
-            sent = select(
-                functools.partial(select_kernel, hop), [pick], [held], flops=10000000000 if hop == 2 else 5000000000
-            )
+        sent = select(
+            functools.partial(select_kernel, hop), [pick], [held], flops=10000000000 if hop == 2 else 5000000000
+        )
+        if hop > 1:
             sent, near[-1] = lax.optimization_barrier((sent, near[-1]))
         if hop == 2:
-            sink = near[0][0, CORES:]
+            sent, along_y = lax.optimization_barrier((sent, along_y))
+            for to, one in enumerate(along_y, 1):
+                sink = jnp.where(y == to, one, sink)
             got = along_rows(sink, (0,), 4)
             onward, q2, q1, q3 = lax.optimization_barrier((onward, q2, q1, q3))
             q1 = along_x(q1, 1)
@@ -430,7 +426,7 @@
         near.append(exchange_y(sent))
         held = onward
     sent = select(select_ends_kernel, [near_first, pick], [own, held])
-    sent, near[-1], got = lax.optimization_barrier((sent, near[-1], got))
+    sent, near[-1], got, q1, q3 = lax.optimization_barrier((sent, near[-1], got, q1, q3))
     sink = jnp.where((z == 2) | (z == 6), got, sink)
     got = along_rows(sink, (0, 2, 4, 6), 1)
     sink = jnp.where((z & 1) == 1, got, sink)

time: 187 us -> 182 us (0.973)
  waiting for transfers between devices: 55.8 us -> 46.3 us
  starting transfers between devices: 71.2 us -> 76.2 us
    ppermute x1 -> x4, starting transfers between devices: 1.29 us -> 8.72 us  [the longest x3 7.43 us: on_device(): lax.ppermute(sink, 'seq', [(c, to * CORES + c) for c in range(CORES)])]
    all_to_all x5, waiting for transfers between devices: 14.2 us -> 8.48 us  [exchange_y(): lax.all_to_all(value, 'seq', split_axis=0, concat_axis=0, axis_index_grou...]
    ppermute x9, starting transfers between devices: 10.7 us -> 15.8 us  [along_x(): lax.ppermute(value, 'mdl', [(i, (i + steps) % MODELS) for i in range(MODE...]
    ppermute x3, starting transfers between devices: 8.88 us -> 5.75 us  [along_rows(): return lax.ppermute(value, 'seq', pairs)]
    ppermute x5, starting transfers between devices: 12.9 us -> 9.78 us  [other_core(): return lax.ppermute(value, 'seq', [(i, i ^ 1) for i in range(count)])]
    ppermute x4, starting transfers between devices: 16.8 us -> 13.7 us  [along_z(): lax.ppermute(value, 'seq', [(i, i + ROW * steps) for i in range(count - R...]
    ppermute x9, waiting for transfers between devices: 26.9 us -> 28.9 us  [along_x(): lax.ppermute(value, 'mdl', [(i, (i + steps) % MODELS) for i in range(MODE...]
    unnamed x30 -> x36, local copies, waits for them, and re-layouts: 8.09 us -> 8.13 us
  transfers between devices with their start and end apart: 27 -> 30, of which waited for: 15 -> 7; matrix products, arithmetic and copies ran while one was open for 4% -> 3% of each run, Pallas kernels for 11% -> 12%
where the time goes in v2:
time: 182 us; the launch traced here: 180 us
  starting transfers between devices  76.2 us (42%)
  waiting for transfers between devices  46.3 us (25%)
  Pallas kernels  43.7 us (24%)
  local copies, waits for them, and re-layouts  9.38 us (5%)
  other arithmetic  4.18 us (2%)
    ppermute x9, waiting for transfers between devices, along_x(): lax.ppermute(value, 'mdl', [(i, (i + steps) % MODELS) for i in range(MODE...  28.9 us
    all_to_all x5, starting transfers between devices, exchange_y(): lax.all_to_all(value, 'seq', split_axis=0, concat_axis=0, axis_index_grou...  22.4 us
    pallas_call x1, Pallas kernels, attend(): pl.pallas_call(attend_kernel, in_specs=[SM, VM] + [HBM] * len(early) + [V...  16.6 us
    ppermute x9, starting transfers between devices, along_x(): lax.ppermute(value, 'mdl', [(i, (i + steps) % MODELS) for i in range(MODE...  15.8 us
    ppermute x4, starting transfers between devices, along_z(): lax.ppermute(value, 'seq', [(i, i + ROW * steps) for i in range(count - R...  13.7 us
    ppermute x5, starting transfers between devices, other_core(): return lax.ppermute(value, 'seq', [(i, i ^ 1) for i in range(count)])  9.78 us
    pallas_call x4, Pallas kernels, select(): pl.pallas_call(body, in_specs=[SM] * len(scalars) + [VM] * len(held), out...  8.61 us
    all_to_all x5, waiting for transfers between devices, exchange_y(): lax.all_to_all(value, 'seq', split_axis=0, concat_axis=0, axis_index_grou...  8.48 us
  transfers between devices with their start and end apart: 30, of which 7 were waited for; matrix products, arithmetic and copies ran while one was open for 3% of the time, Pallas kernels for 12%

profile of v2, /device:TPU:1, one launch (start us, length us, event | category | flops | bytes accessed | tf_op | source)
XLA Modules:
  0.0 180.4 jit_solution(11274579232497199850)
XLA Ops:
  0.0 2.5 %split_columns.3 = (bf16[256,1024]{1,0:T(8,128)(2,1)}, bf16[256,1024]{1,0:T(8,128)(2,1)}, bf16[256,1024]{1,0:T(8,128)(2,1)}) custom-call(s32[1]{0:T(128)} %bitcast.rank_ref, bf16[256,4096]{1,0:T(8,128)(2,1)} %tokens.3), custom_call_target="tpu_custom_call" | custom-call | flops 1 | bytes 1 | tf_op jit(solution)/shard_map/split_columns/pallas_call | solution.py:79
  2.5 2.1 %collective-permute-start = (bf16[256,1024]{1,0:T(8,128)(2,1)}, bf16[256,1024]{1,0:T(8,128)(2,1)}, u32[]{:S(2)}, u32[]{:S(2)}) collective-permute-start(bf16[256,1024]{1,0:T(8,128)(2,1)} %get-tuple-element.67), channel_id=1, source_target_pairs={{0,1},{1,2},{2,3},{3,0},{4,5},{5,6},{6,7},{7,4},{8,9},{9,10},{10,1... | collective-permute-start | bytes 1572872 | tf_op jit(solution)/shard_map/ppermute | solution.py:34
  4.7 2.5 %collective-permute-start.1 = (bf16[256,1024]{1,0:T(8,128)(2,1)}, bf16[256,1024]{1,0:T(8,128)(2,1)}, u32[]{:S(2)}, u32[]{:S(2)}) collective-permute-start(bf16[256,1024]{1,0:T(8,128)(2,1)} %get-tuple-element.68), channel_id=1, source_target_pairs={{0,2},{1,3},{2,0},{3,1},{4,6},{5,7},{6,4},{7,5},{8,10},{9,11},{10,... | collective-permute-start | bytes 1572872 | tf_op jit(solution)/shard_map/ppermute | solution.py:34
  7.1 1.2 collective-permute-start.2
  8.9 1.6 collective-permute-start.3
  10.5 1.9 %fusion = (f32[1024,64]{1,0:T(8,128)S(1)}, f32[1024,64]{1,0:T(8,128)S(1)}, f32[1024,64]{1,0:T(8,128)S(1)}) fusion(f32[64]{0:T(128)S(1)} %multiply_power_fusion, f32[1024]{0:T(1024)S(1)} %add_convert_fusion), kind=kLoop, calls=%fused_computation.4 | loop fusion | flops 131072 | bytes 790784 | tf_op jit(solution)/shard_map/neg | solution.py:345
  14.2 4.2 %all-to-all-start = ((s32[4,2,5,8]{3,1,2,0:T(2,128)}), s32[4,2,5,8]{3,1,2,0:T(2,128)S(1)}, u32[]{:S(2)}, u32[]{:S(2)}) async-start(s32[4,2,5,8]{3,1,2,0:T(2,128)} %broadcast_in_dim.30), calls=%async_computation | async-start | bytes 40960 | tf_op jit(solution)/shard_map/all_to_all | solution.py:52
  19.4 1.2 copy-done.4
  20.6 1.2 copy-done.5
  23.2 6.8 %collective-permute-done.1.t2 = bf16[256,1024]{1,0:T(8,128)(2,1)} collective-permute-done((bf16[256,1024]{1,0:T(8,128)(2,1)}, bf16[256,1024]{1,0:T(8,128)(2,1)}, u32[]{:S(2)}, u32[]{:S(2)}) %collective-permute-start.1) | collective-permute-done | bytes 524320 | tf_op jit(solution)/shard_map/ppermute | solution.py:34
  30.0 3.3 %kv_parts.2 = (bf16[1024,256]{1,0:T(8,128)(2,1)S(1)}, bf16[1024,256]{1,0:T(8,128)(2,1)S(1)}, bf16[1024,256]{1,0:T(8,128)(2,1)S(1)}) custom-call(s32[1]{0:T(128)} %bitcast.rank_ref, bf16[256,1024]{1,0:T(8,128)(2,1)S(1)} %split_columns.2.t0, bf16[256,1024]{1,0:T(8,128)(2,1)} %collective-permute-done.t1, bf16[256,1024]{1,0:T(8,128)(2,1)} %collective-permute-done.1.t2, ...), custom_call_target="tpu_custom_call" | custom-call | flops 1 | bytes 1 | tf_op jit(solution)/shard_map/kv_parts/pallas_call | solution.py:124
  33.3 1.2 collective-permute-start.4
  34.6 3.0 %collective-permute-start.5 = (bf16[1024,256]{1,0:T(8,128)(2,1)S(1)}, bf16[1024,256]{1,0:T(8,128)(2,1)S(1)}, u32[]{:S(2)}, u32[]{:S(2)}) collective-permute-start(bf16[1024,256]{1,0:T(8,128)(2,1)S(1)} %get-tuple-element.82), channel_id=1, source_target_pairs={{0,2},{1,3},{2,0},{3,1},{4,6},{5,7},{6,4},{7,5},{8,10},{9,11},{10,... | collective-permute-start | bytes 1572872 | tf_op jit(solution)/shard_map/ppermute | solution.py:34
  37.6 5.9 %query_parts.1 = (bf16[1024,512]{1,0:T(8,128)(2,1)S(1)}, bf16[1024,512]{1,0:T(8,128)(2,1)S(1)}, bf16[1024,512]{1,0:T(8,128)(2,1)S(1)}, bf16[1024,512]{1,0:T(8,128)(2,1)S(1)}) custom-call(s32[1]{0:T(128)} %bitcast.rank_ref, bf16[256,1024]{1,0:T(8,128)(2,1)S(1)} %split_columns.2.t0, bf16[256,1024]{1,0:T(8,128)(2,1)} %collective-permute-done.t1, ...), custom_call_target="tpu_custom_call" | custom-call | flops 1 | bytes 1 | tf_op jit(solution)/shard_map/query_parts/pallas_call | solution.py:149
  45.5 2.9 %kv_parts.3.own = f32[1024,256]{1,0:T(8,128)S(1)} custom-call(s32[1]{0:T(128)} %bitcast.rank_ref, bf16[256,1024]{1,0:T(8,128)(2,1)S(1)} %split_columns.2.t0, bf16[256,1024]{1,0:T(8,128)(2,1)} %collective-permute-done.t1, bf16[256,1024]{1,0:T(8,128)(2,1)} %collective-permute-done.1.t2, bf16[256,1024]{1,0:T(8,128)(2,1)} %collective-permute-done.2.t3, ...), custom_call_target="tpu_custom_call" | custom-call | flops 1 | bytes 1 | tf_op jit(solution)/shard_map/kv_parts/pallas_call | solution.py:124
  48.4 11.9 %collective-permute-done.5.b = bf16[1024,256]{1,0:T(8,128)(2,1)S(1)} collective-permute-done((bf16[1024,256]{1,0:T(8,128)(2,1)S(1)}, bf16[1024,256]{1,0:T(8,128)(2,1)S(1)}, u32[]{:S(2)}, u32[]{:S(2)}) %collective-permute-start.5) | collective-permute-done | bytes 524320 | tf_op jit(solution)/shard_map/ppermute | solution.py:34
  60.7 4.5 %collective-permute-start.7 = (bf16[4,256,256]{2,1,0:T(8,128)(2,1)S(1)}, bf16[4,256,256]{2,1,0:T(8,128)(2,1)}, u32[]{:S(2)}, u32[]{:S(2)}) collective-permute-start(bf16[4,256,256]{2,1,0:T(8,128)(2,1)S(1)} %bitcast.9), channel_id=1, source_target_pairs={{0,32},{4,36},{8,40},{12,44},{16,48},{20,52},{24,56},{28,60},{32,6... | collective-permute-start | bytes 1572872 | tf_op jit(solution)/shard_map/ppermute | solution.py:39
  65.1 1.3 collective-permute-start.12
  67.5 6.7 %collective-permute-done.7.held = bf16[4,256,256]{2,1,0:T(8,128)(2,1)} collective-permute-done((bf16[4,256,256]{2,1,0:T(8,128)(2,1)S(1)}, bf16[4,256,256]{2,1,0:T(8,128)(2,1)}, u32[]{:S(2)}, u32[]{:S(2)}) %collective-permute-start.7) | collective-permute-done | bytes 524320 | tf_op jit(solution)/shard_map/ppermute | solution.py:39
  74.2 5.0 %collective-permute-start.8 = (bf16[4,256,256]{2,1,0:T(8,128)(2,1)}, bf16[4,256,256]{2,1,0:T(8,128)(2,1)}, u32[]{:S(2)}, u32[]{:S(2)}) collective-permute-start(bf16[4,256,256]{2,1,0:T(8,128)(2,1)} %collective-permute-done.7.held), channel_id=1, source_target_pairs={{0,32},{4,36},{8,40},{12,44},{16,48},{20,52},{24,56},{28,60},{32,6... | collective-permute-start | bytes 1572872 | tf_op jit(solution)/shard_map/ppermute | solution.py:39
  79.2 3.2 %collective-permute-start.13 = (bf16[1,256,256]{2,1,0:T(8,128)(2,1)S(1)}, bf16[1,256,256]{2,1,0:T(8,128)(2,1)S(1)}, u32[]{:S(2)}, u32[]{:S(2)}) collective-permute-start(bf16[1,256,256]{2,1,0:T(8,128)(2,1)S(1)} %broadcast_select_fusion.3), channel_id=1, source_target_pairs={{0,8},{4,12},{1,9},{5,13},{2,10},{6,14},{3,11},{7,15}} | collective-permute-start | bytes 393224 | tf_op jit(solution)/shard_map/ppermute | solution.py:405
  82.4 2.3 %collective-permute-start.14 = (bf16[1,256,256]{2,1,0:T(8,128)(2,1)S(1)}, bf16[1,256,256]{2,1,0:T(8,128)(2,1)S(1)}, u32[]{:S(2)}, u32[]{:S(2)}) collective-permute-start(bf16[1,256,256]{2,1,0:T(8,128)(2,1)S(1)} %broadcast_select_fusion.3), channel_id=1, source_target_pairs={{0,16},{4,20},{1,17},{5,21},{2,18},{6,22},{3,19},{7,23}} | collective-permute-start | bytes 393224 | tf_op jit(solution)/shard_map/ppermute | solution.py:405
  84.7 1.9 %collective-permute-start.15 = (bf16[1,256,256]{2,1,0:T(8,128)(2,1)S(1)}, bf16[1,256,256]{2,1,0:T(8,128)(2,1)}, u32[]{:S(2)}, u32[]{:S(2)}) collective-permute-start(bf16[1,256,256]{2,1,0:T(8,128)(2,1)S(1)} %broadcast_select_fusion.3), channel_id=1, source_target_pairs={{0,24},{4,28},{1,25},{5,29},{2,26},{6,30},{3,27},{7,31}} | collective-permute-start | bytes 393224 | tf_op jit(solution)/shard_map/ppermute | solution.py:405
  86.6 2.1 %select_blocks.7 = bf16[4,2,256,256]{3,2,1,0:T(8,128)(2,1)} custom-call(s32[5,8]{1,0:T(8,128)S(1)} %copy.19.pick_ref, bf16[4,256,256]{2,1,0:T(8,128)(2,1)} %collective-permute-done.7.held), custom_call_target="tpu_custom_call" | custom-call | flops 5000000000 | bytes 1 | tf_op jit(solution)/shard_map/select_blocks/pallas_call | solution.py:238
  88.7 4.2 %all-to-all-start.1 = ((bf16[4,2,256,256]{3,2,1,0:T(8,128)(2,1)}), bf16[4,2,256,256]{3,2,1,0:T(8,128)(2,1)}, u32[]{:S(2)}, u32[]{:S(2)}) async-start(bf16[4,2,256,256]{3,2,1,0:T(8,128)(2,1)} %select_blocks.7), calls=%async_computation.1 | async-start | bytes 2097152 | tf_op jit(solution)/shard_map/all_to_all | solution.py:52
  93.0 2.1 %collective-permute-start.9 = (bf16[4,256,256]{2,1,0:T(8,128)(2,1)}, bf16[4,256,256]{2,1,0:T(8,128)(2,1)}, u32[]{:S(2)}, u32[]{:S(2)}) collective-permute-start(bf16[4,256,256]{2,1,0:T(8,128)(2,1)} %collective-permute-done.8.held), channel_id=1, source_target_pairs={{0,32},{4,36},{8,40},{12,44},{16,48},{20,52},{24,56},{28,60},{32,6... | collective-permute-start | bytes 1572872 | tf_op jit(solution)/shard_map/ppermute | solution.py:39
  95.1 2.1 %select_blocks.6 = bf16[4,2,256,256]{3,2,1,0:T(8,128)(2,1)} custom-call(s32[5,8]{1,0:T(8,128)S(1)} %copy.19.pick_ref, bf16[4,256,256]{2,1,0:T(8,128)(2,1)} %collective-permute-done.8.held), custom_call_target="tpu_custom_call" | custom-call | flops 10000000000 | bytes 1 | tf_op jit(solution)/shard_map/select_blocks/pallas_call | solution.py:238
  97.3 7.8 %all-to-all-done.1.refs_0_ = bf16[4,2,256,256]{3,2,1,0:T(8,128)(2,1)} async-done(((bf16[4,2,256,256]{3,2,1,0:T(8,128)(2,1)}), bf16[4,2,256,256]{3,2,1,0:T(8,128)(2,1)}, u32[]{:S(2)}, u32[]{:S(2)}) %all-to-all-start.1) | async-done | bytes 1048608 | tf_op jit(solution)/shard_map/all_to_all | solution.py:52
  105.1 4.2 %all-to-all-start.2 = ((bf16[4,2,256,256]{3,2,1,0:T(8,128)(2,1)}), bf16[4,2,256,256]{3,2,1,0:T(8,128)(2,1)}, u32[]{:S(2)}, u32[]{:S(2)}) async-start(bf16[4,2,256,256]{3,2,1,0:T(8,128)(2,1)} %select_blocks.6), calls=%async_computation.2 | async-start | bytes 2097152 | tf_op jit(solution)/shard_map/all_to_all | solution.py:52
  109.4 3.2 %collective-permute-start.16 = (bf16[1,256,256]{2,1,0:T(8,128)(2,1)S(1)}, bf16[1,256,256]{2,1,0:T(8,128)(2,1)S(1)}, u32[]{:S(2)}, u32[]{:S(2)}) collective-permute-start(bf16[1,256,256]{2,1,0:T(8,128)(2,1)S(1)} %select_select_fusion), channel_id=1, source_target_pairs={{0,128},{4,132},{8,136},{12,140},{16,144},{20,148},{24,152},{28,15... | collective-permute-start | bytes 393224 | tf_op jit(solution)/shard_map/ppermute | solution.py:44
  112.6 2.1 %collective-permute-start.11 = (bf16[4,256,256]{2,1,0:T(8,128)(2,1)}, bf16[4,256,256]{2,1,0:T(8,128)(2,1)}, u32[]{:S(2)}, u32[]{:S(2)}) collective-permute-start(bf16[4,256,256]{2,1,0:T(8,128)(2,1)} %collective-permute-done.9.held), channel_id=1, source_target_pairs={{0,32},{4,36},{8,40},{12,44},{16,48},{20,52},{24,56},{28,60},{32,6... | collective-permute-start | bytes 1572872 | tf_op jit(solution)/shard_map/ppermute | solution.py:39
  114.7 3.5 %collective-permute-start.18 = (bf16[1024,512]{1,0:T(8,128)(2,1)}, bf16[1024,512]{1,0:T(8,128)(2,1)S(1)}, u32[]{:S(2)}, u32[]{:S(2)}) collective-permute-start(bf16[1024,512]{1,0:T(8,128)(2,1)} %copy-done.13), channel_id=1, source_target_pairs={{0,1},{1,2},{2,3},{3,0},{4,5},{5,6},{6,7},{7,4},{8,9},{9,10},{10,1... | collective-permute-start | bytes 3145736 | tf_op jit(solution)/shard_map/ppermute | solution.py:34
  118.3 1.4 collective-permute-start.19
  119.6 2.1 %select_blocks.5 = bf16[4,2,256,256]{3,2,1,0:T(8,128)(2,1)} custom-call(s32[5,8]{1,0:T(8,128)S(1)} %copy.19.pick_ref, bf16[4,256,256]{2,1,0:T(8,128)(2,1)} %collective-permute-done.9.held), custom_call_target="tpu_custom_call" | custom-call | flops 5000000000 | bytes 1 | tf_op jit(solution)/shard_map/select_blocks/pallas_call | solution.py:238
  121.7 5.1 %all-to-all-start.3 = ((bf16[4,2,256,256]{3,2,1,0:T(8,128)(2,1)}), bf16[4,2,256,256]{3,2,1,0:T(8,128)(2,1)}, u32[]{:S(2)}, u32[]{:S(2)}) async-start(bf16[4,2,256,256]{3,2,1,0:T(8,128)(2,1)} %select_blocks.5), calls=%async_computation.3 | async-start | bytes 2097152 | tf_op jit(solution)/shard_map/all_to_all | solution.py:52
  126.8 1.3 collective-permute-start.17
  128.1 2.3 %select_blocks.4 = bf16[4,2,256,256]{3,2,1,0:T(8,128)(2,1)} custom-call(s32[4]{0:T(128)S(1)} %or_convert_fusion.near_ref, s32[5,8]{1,0:T(8,128)S(1)} %copy.19.pick_ref, bf16[4,256,256]{2,1,0:T(8,128)(2,1)S(1)} %bitcast.12, bf16[4,256,256]{2,1,0:T(8,128)(2,1)} %collective-permute-done.11.last), custom_call_target="tpu_custom_call" | custom-call | flops 5000000000 | bytes 1 | tf_op jit(solution)/shard_map/select_blocks/pallas_call | solution.py:238
  130.4 10.2 %collective-permute-done.18.b = bf16[1024,512]{1,0:T(8,128)(2,1)S(1)} collective-permute-done((bf16[1024,512]{1,0:T(8,128)(2,1)}, bf16[1024,512]{1,0:T(8,128)(2,1)S(1)}, u32[]{:S(2)}, u32[]{:S(2)}) %collective-permute-start.18) | collective-permute-done | bytes 1048608 | tf_op jit(solution)/shard_map/ppermute | solution.py:34
  140.6 4.7 %all-to-all-start.4 = ((bf16[4,2,256,256]{3,2,1,0:T(8,128)(2,1)}), bf16[4,2,256,256]{3,2,1,0:T(8,128)(2,1)S(1)}, u32[]{:S(2)}, u32[]{:S(2)}) async-start(bf16[4,2,256,256]{3,2,1,0:T(8,128)(2,1)} %select_blocks.4), calls=%async_computation.4 | async-start | bytes 2097152 | tf_op jit(solution)/shard_map/all_to_all | solution.py:52
  145.3 1.3 collective-permute-start.20
  146.6 4.3 %collective-permute-start.21 = (bf16[4,2,256,256]{3,2,1,0:T(8,128)(2,1)}, bf16[4,2,256,256]{3,2,1,0:T(8,128)(2,1)}, u32[]{:S(2)}, u32[]{:S(2)}) collective-permute-start(bf16[4,2,256,256]{3,2,1,0:T(8,128)(2,1)} %all-to-all-done.1.refs_0_), channel_id=1, source_target_pairs={{0,4},{4,0},{8,12},{12,8},{16,20},{20,16},{24,28},{28,24},{32,36},... | collective-permute-start | bytes 3145736 | tf_op jit(solution)/shard_map/ppermute | solution.py:57
  151.4 1.2 copy-done.7
  152.6 1.2 copy-done.9
  153.9 1.2 copy-done.11
  155.1 2.2 %q_join.1.query = bf16[1024,512]{1,0:T(8,128)(2,1)S(1)} custom-call(bf16[1024,512]{1,0:T(8,128)(2,1)S(1)} %copy-done.7, bf16[1024,512]{1,0:T(8,128)(2,1)S(1)} %copy-done.11, bf16[1024,512]{1,0:T(8,128)(2,1)S(1)} %copy-done.9, bf16[1024,512]{1,0:T(8,128)(2,1)} %collective-permute-done.19.d, f32[1024,128]{1,0:T(8,128)S(1)} %get-tuple-element.93.cosine, ...), custom_call_target="tpu_custom_call" | custom-call | flops 1 | bytes 1 | tf_op jit(solution)/shard_map/q_join/pallas_call | solution.py:206
  158.0 3.4 %collective-permute-start.24 = (bf16[4,2,256,256]{3,2,1,0:T(8,128)(2,1)S(1)}, bf16[4,2,256,256]{3,2,1,0:T(8,128)(2,1)S(1)}, u32[]{:S(2)}, u32[]{:S(2)}) collective-permute-start(bf16[4,2,256,256]{3,2,1,0:T(8,128)(2,1)S(1)} %all-to-all-done.4.refs_6_), channel_id=1, source_target_pairs={{0,4},{4,0},{8,12},{12,8},{16,20},{20,16},{24,28},{28,24},{32,36},... | collective-permute-start | bytes 3145736 | tf_op jit(solution)/shard_map/ppermute | solution.py:57
  161.4 2.3 %collective-permute-done.24.refs_7_ = bf16[4,2,256,256]{3,2,1,0:T(8,128)(2,1)S(1)} collective-permute-done((bf16[4,2,256,256]{3,2,1,0:T(8,128)(2,1)S(1)}, bf16[4,2,256,256]{3,2,1,0:T(8,128)(2,1)S(1)}, u32[]{:S(2)}, u32[]{:S(2)}) %collective-permute-start.24) | collective-permute-done | bytes 1048608 | tf_op jit(solution)/shard_map/ppermute | solution.py:57
  163.6 16.6 %attend.1 = bf16[1024,512]{1,0:T(8,128)(2,1)} custom-call(s32[32]{0:T(128)S(1)} %reshape.71.index_ref, bf16[1024,512]{1,0:T(8,128)(2,1)S(1)} %q_join.1.query, bf16[4,256,256]{2,1,0:T(8,128)(2,1)} %bitcast.13, bf16[1,256,256]{2,1,0:T(8,128)(2,1)} %broadcast_select_fusion.1.sink, bf16[4,2,256,256]{3,2,1,0:T(8,128)(2,1)} %all-to-all-done.1.refs_0_, ...), custom_call_target="tpu_custom_call" | custom-call | flops 1 | bytes 1 | tf_op jit(solution)/shard_map/attend/pallas_call | solution.py:324
  (87 shorter events, 9.6 us)
Async XLA Ops:
  0.0 8.3 %copy-start.17 = (s32[4,8]{1,0:T(4,128)S(1)}, s32[4,8]{1,0:T(4,128)}, u32[]{:S(2)}) copy-start(s32[4,8]{1,0:T(4,128)} %param.9) | copy-start | bytes 388
  2.5 20.7 %collective-permute-start = (bf16[256,1024]{1,0:T(8,128)(2,1)}, bf16[256,1024]{1,0:T(8,128)(2,1)}, u32[]{:S(2)}, u32[]{:S(2)}) collective-permute-start(bf16[256,1024]{1,0:T(8,128)(2,1)} %get-tuple-element.67), channel_id=1, source_target_pairs={{0,1},{1,2},{2,3},{3,0},{4,5},{5,6},{6,7},{7,4},{8,9},{9,10},{10,1... | collective-permute-start | bytes 1572872 | tf_op jit(solution)/shard_map/ppermute | solution.py:34
  4.7 25.3 %collective-permute-start.1 = (bf16[256,1024]{1,0:T(8,128)(2,1)}, bf16[256,1024]{1,0:T(8,128)(2,1)}, u32[]{:S(2)}, u32[]{:S(2)}) collective-permute-start(bf16[256,1024]{1,0:T(8,128)(2,1)} %get-tuple-element.68), channel_id=1, source_target_pairs={{0,2},{1,3},{2,0},{3,1},{4,6},{5,7},{6,4},{7,5},{8,10},{9,11},{10,... | collective-permute-start | bytes 1572872 | tf_op jit(solution)/shard_map/ppermute | solution.py:34
  7.1 22.9 %collective-permute-start.2 = (bf16[256,1024]{1,0:T(8,128)(2,1)}, bf16[256,1024]{1,0:T(8,128)(2,1)}, u32[]{:S(2)}, u32[]{:S(2)}) collective-permute-start(bf16[256,1024]{1,0:T(8,128)(2,1)} %get-tuple-element.69), channel_id=1, source_target_pairs={{0,3},{1,0},{2,1},{3,2},{4,7},{5,4},{6,5},{7,6},{8,11},{9,8},{10,9... | collective-permute-start | bytes 1572872 | tf_op jit(solution)/shard_map/ppermute | solution.py:34
  8.9 4.7 %collective-permute-start.3 = (s32[5,8]{1,0:T(8,128)S(1)}, s32[5,8]{1,0:T(8,128)S(1)}, u32[]{:S(2)}, u32[]{:S(2)}) collective-permute-start(s32[5,8]{1,0:T(8,128)S(1)} %select_reduce_fusion), channel_id=1, source_target_pairs={{0,4},{4,0},{8,12},{12,8},{16,20},{20,16},{24,28},{28,24},{32,36},... | collective-permute-start | bytes 488 | tf_op jit(solution)/shard_map/ppermute | solution.py:57
  14.2 8.8 %all-to-all-start = ((s32[4,2,5,8]{3,1,2,0:T(2,128)}), s32[4,2,5,8]{3,1,2,0:T(2,128)S(1)}, u32[]{:S(2)}, u32[]{:S(2)}) async-start(s32[4,2,5,8]{3,1,2,0:T(2,128)} %broadcast_in_dim.30), calls=%async_computation | async-start | bytes 40960 | tf_op jit(solution)/shard_map/all_to_all | solution.py:52
  19.4 1.2 copy-start.4
  20.6 1.2 copy-start.5
  30.0 7.6 %copy-start.2 = (bf16[1024,2048]{1,0:T(8,128)(2,1)S(1)}, bf16[1024,2048]{1,0:T(8,128)(2,1)}, u32[]{:S(2)}) copy-start(bf16[1024,2048]{1,0:T(8,128)(2,1)} %wq.1) | copy-start | bytes 12582916
  33.3 15.1 %collective-permute-start.4 = (bf16[1024,256]{1,0:T(8,128)(2,1)S(1)}, bf16[1024,256]{1,0:T(8,128)(2,1)S(1)}, u32[]{:S(2)}, u32[]{:S(2)}) collective-permute-start(bf16[1024,256]{1,0:T(8,128)(2,1)S(1)} %get-tuple-element.80), channel_id=1, source_target_pairs={{0,1},{1,2},{2,3},{3,0},{4,5},{5,6},{6,7},{7,4},{8,9},{9,10},{10,1... | collective-permute-start | bytes 1572872 | tf_op jit(solution)/shard_map/ppermute | solution.py:34
  34.6 25.7 %collective-permute-start.5 = (bf16[1024,256]{1,0:T(8,128)(2,1)S(1)}, bf16[1024,256]{1,0:T(8,128)(2,1)S(1)}, u32[]{:S(2)}, u32[]{:S(2)}) collective-permute-start(bf16[1024,256]{1,0:T(8,128)(2,1)S(1)} %get-tuple-element.82), channel_id=1, source_target_pairs={{0,2},{1,3},{2,0},{3,1},{4,6},{5,7},{6,4},{7,5},{8,10},{9,11},{10,... | collective-permute-start | bytes 1572872 | tf_op jit(solution)/shard_map/ppermute | solution.py:34
  37.5 22.8 %collective-permute-start.6 = (bf16[1024,256]{1,0:T(8,128)(2,1)S(1)}, bf16[1024,256]{1,0:T(8,128)(2,1)S(1)}, u32[]{:S(2)}, u32[]{:S(2)}) collective-permute-start(bf16[1024,256]{1,0:T(8,128)(2,1)S(1)} %get-tuple-element.83), channel_id=1, source_target_pairs={{0,3},{1,0},{2,1},{3,2},{4,7},{5,4},{6,5},{7,6},{8,11},{9,8},{10,9... | collective-permute-start | bytes 1572872 | tf_op jit(solution)/shard_map/ppermute | solution.py:34
  43.5 1.0 copy-start.6
  44.5 1.0 copy-start.14
  45.5 2.9 %copy-start.12 = (bf16[1024,512]{1,0:T(8,128)(2,1)}, bf16[1024,512]{1,0:T(8,128)(2,1)S(1)}, u32[]{:S(2)}) copy-start(bf16[1024,512]{1,0:T(8,128)(2,1)S(1)} %get-tuple-element.110) | copy-start | bytes 3145732
  45.5 2.9 %copy-start.13 = (bf16[1024,512]{1,0:T(8,128)(2,1)}, bf16[1024,512]{1,0:T(8,128)(2,1)S(1)}, u32[]{:S(2)}) copy-start(bf16[1024,512]{1,0:T(8,128)(2,1)S(1)} %get-tuple-element.109) | copy-start | bytes 3145732
  45.5 14.8 %copy-start = (f32[1024,128]{1,0:T(8,128)S(1)}, f32[1024,128]{1,0:T(8,128)}, u32[]{:S(2)}) copy-start(f32[1024,128]{1,0:T(8,128)} %get-tuple-element.94.sine) | copy-start | bytes 1572868
  48.4 18.1 %copy-start.15 = (bf16[1024,512]{1,0:T(8,128)(2,1)S(1)}, bf16[1024,512]{1,0:T(8,128)(2,1)}, u32[]{:S(2)}) copy-start(bf16[1024,512]{1,0:T(8,128)(2,1)} %copy-done.14) | copy-start | bytes 3145732
  60.7 67.5 %copy-start.3 = (bf16[1024,256]{1,0:T(8,128)(2,1)}, bf16[1024,256]{1,0:T(8,128)(2,1)S(1)}, u32[]{:S(2)}) copy-start(bf16[1024,256]{1,0:T(8,128)(2,1)S(1)} %kv_join.1) | copy-start | bytes 1572868
  60.7 13.5 %collective-permute-start.7 = (bf16[4,256,256]{2,1,0:T(8,128)(2,1)S(1)}, bf16[4,256,256]{2,1,0:T(8,128)(2,1)}, u32[]{:S(2)}, u32[]{:S(2)}) collective-permute-start(bf16[4,256,256]{2,1,0:T(8,128)(2,1)S(1)} %bitcast.9), channel_id=1, source_target_pairs={{0,32},{4,36},{8,40},{12,44},{16,48},{20,52},{24,56},{28,60},{32,6... | collective-permute-start | bytes 1572872 | tf_op jit(solution)/shard_map/ppermute | solution.py:39
  65.1 14.0 %collective-permute-start.12 = (bf16[1,256,256]{2,1,0:T(8,128)(2,1)S(1)}, bf16[1,256,256]{2,1,0:T(8,128)(2,1)S(1)}, u32[]{:S(2)}, u32[]{:S(2)}) collective-permute-start(bf16[1,256,256]{2,1,0:T(8,128)(2,1)S(1)} %slice.4), channel_id=1, source_target_pairs={{0,4},{1,5},{2,6},{3,7}} | collective-permute-start | bytes 393224 | tf_op jit(solution)/shard_map/ppermute | solution.py:404
  66.5 46.1 %collective-permute-start.10 = (bf16[1024,512]{1,0:T(8,128)(2,1)S(1)}, bf16[1024,512]{1,0:T(8,128)(2,1)S(1)}, u32[]{:S(2)}, u32[]{:S(2)}) collective-permute-start(bf16[1024,512]{1,0:T(8,128)(2,1)S(1)} %copy-done.15), channel_id=1, source_target_pairs={{0,2},{1,3},{2,0},{3,1},{4,6},{5,7},{6,4},{7,5},{8,10},{9,11},{10,... | collective-permute-start | bytes 3145736 | tf_op jit(solution)/shard_map/ppermute | solution.py:34
  74.2 18.8 %collective-permute-start.8 = (bf16[4,256,256]{2,1,0:T(8,128)(2,1)}, bf16[4,256,256]{2,1,0:T(8,128)(2,1)}, u32[]{:S(2)}, u32[]{:S(2)}) collective-permute-start(bf16[4,256,256]{2,1,0:T(8,128)(2,1)} %collective-permute-done.7.held), channel_id=1, source_target_pairs={{0,32},{4,36},{8,40},{12,44},{16,48},{20,52},{24,56},{28,60},{32,6... | collective-permute-start | bytes 1572872 | tf_op jit(solution)/shard_map/ppermute | solution.py:39
  79.2 25.9 %collective-permute-start.13 = (bf16[1,256,256]{2,1,0:T(8,128)(2,1)S(1)}, bf16[1,256,256]{2,1,0:T(8,128)(2,1)S(1)}, u32[]{:S(2)}, u32[]{:S(2)}) collective-permute-start(bf16[1,256,256]{2,1,0:T(8,128)(2,1)S(1)} %broadcast_select_fusion.3), channel_id=1, source_target_pairs={{0,8},{4,12},{1,9},{5,13},{2,10},{6,14},{3,11},{7,15}} | collective-permute-start | bytes 393224 | tf_op jit(solution)/shard_map/ppermute | solution.py:405
  82.4 22.7 %collective-permute-start.14 = (bf16[1,256,256]{2,1,0:T(8,128)(2,1)S(1)}, bf16[1,256,256]{2,1,0:T(8,128)(2,1)S(1)}, u32[]{:S(2)}, u32[]{:S(2)}) collective-permute-start(bf16[1,256,256]{2,1,0:T(8,128)(2,1)S(1)} %broadcast_select_fusion.3), channel_id=1, source_target_pairs={{0,16},{4,20},{1,17},{5,21},{2,18},{6,22},{3,19},{7,23}} | collective-permute-start | bytes 393224 | tf_op jit(solution)/shard_map/ppermute | solution.py:405
  84.7 20.4 %collective-permute-start.15 = (bf16[1,256,256]{2,1,0:T(8,128)(2,1)S(1)}, bf16[1,256,256]{2,1,0:T(8,128)(2,1)}, u32[]{:S(2)}, u32[]{:S(2)}) collective-permute-start(bf16[1,256,256]{2,1,0:T(8,128)(2,1)S(1)} %broadcast_select_fusion.3), channel_id=1, source_target_pairs={{0,24},{4,28},{1,25},{5,29},{2,26},{6,30},{3,27},{7,31}} | collective-permute-start | bytes 393224 | tf_op jit(solution)/shard_map/ppermute | solution.py:405
  88.7 16.3 %all-to-all-start.1 = ((bf16[4,2,256,256]{3,2,1,0:T(8,128)(2,1)}), bf16[4,2,256,256]{3,2,1,0:T(8,128)(2,1)}, u32[]{:S(2)}, u32[]{:S(2)}) async-start(bf16[4,2,256,256]{3,2,1,0:T(8,128)(2,1)} %select_blocks.7), calls=%async_computation.1 | async-start | bytes 2097152 | tf_op jit(solution)/shard_map/all_to_all | solution.py:52
  93.0 19.6 %collective-permute-start.9 = (bf16[4,256,256]{2,1,0:T(8,128)(2,1)}, bf16[4,256,256]{2,1,0:T(8,128)(2,1)}, u32[]{:S(2)}, u32[]{:S(2)}) collective-permute-start(bf16[4,256,256]{2,1,0:T(8,128)(2,1)} %collective-permute-done.8.held), channel_id=1, source_target_pairs={{0,32},{4,36},{8,40},{12,44},{16,48},{20,52},{24,56},{28,60},{32,6... | collective-permute-start | bytes 1572872 | tf_op jit(solution)/shard_map/ppermute | solution.py:39
  105.1 4.3 %copy-start.16 = (bf16[1,256,256]{2,1,0:T(8,128)(2,1)}, bf16[1,256,256]{2,1,0:T(8,128)(2,1)S(1)}, u32[]{:S(2)}) copy-start(bf16[1,256,256]{2,1,0:T(8,128)(2,1)S(1)} %collective-permute-done.14) | copy-start | bytes 393220
  105.1 16.6 %all-to-all-start.2 = ((bf16[4,2,256,256]{3,2,1,0:T(8,128)(2,1)}), bf16[4,2,256,256]{3,2,1,0:T(8,128)(2,1)}, u32[]{:S(2)}, u32[]{:S(2)}) async-start(bf16[4,2,256,256]{3,2,1,0:T(8,128)(2,1)} %select_blocks.6), calls=%async_computation.2 | async-start | bytes 2097152 | tf_op jit(solution)/shard_map/all_to_all | solution.py:52
  109.4 12.3 %collective-permute-start.16 = (bf16[1,256,256]{2,1,0:T(8,128)(2,1)S(1)}, bf16[1,256,256]{2,1,0:T(8,128)(2,1)S(1)}, u32[]{:S(2)}, u32[]{:S(2)}) collective-permute-start(bf16[1,256,256]{2,1,0:T(8,128)(2,1)S(1)} %select_select_fusion), channel_id=1, source_target_pairs={{0,128},{4,132},{8,136},{12,140},{16,144},{20,148},{24,152},{28,15... | collective-permute-start | bytes 393224 | tf_op jit(solution)/shard_map/ppermute | solution.py:44
  112.6 9.1 %copy-start.8 = (bf16[1024,512]{1,0:T(8,128)(2,1)}, bf16[1024,512]{1,0:T(8,128)(2,1)S(1)}, u32[]{:S(2)}) copy-start(bf16[1024,512]{1,0:T(8,128)(2,1)S(1)} %collective-permute-done.10.c) | copy-start | bytes 3145732
  112.6 15.5 %collective-permute-start.11 = (bf16[4,256,256]{2,1,0:T(8,128)(2,1)}, bf16[4,256,256]{2,1,0:T(8,128)(2,1)}, u32[]{:S(2)}, u32[]{:S(2)}) collective-permute-start(bf16[4,256,256]{2,1,0:T(8,128)(2,1)} %collective-permute-done.9.held), channel_id=1, source_target_pairs={{0,32},{4,36},{8,40},{12,44},{16,48},{20,52},{24,56},{28,60},{32,6... | collective-permute-start | bytes 1572872 | tf_op jit(solution)/shard_map/ppermute | solution.py:39
  114.7 25.9 %collective-permute-start.18 = (bf16[1024,512]{1,0:T(8,128)(2,1)}, bf16[1024,512]{1,0:T(8,128)(2,1)S(1)}, u32[]{:S(2)}, u32[]{:S(2)}) collective-permute-start(bf16[1024,512]{1,0:T(8,128)(2,1)} %copy-done.13), channel_id=1, source_target_pairs={{0,1},{1,2},{2,3},{3,0},{4,5},{5,6},{6,7},{7,4},{8,9},{9,10},{10,1... | collective-permute-start | bytes 3145736 | tf_op jit(solution)/shard_map/ppermute | solution.py:34
  118.3 22.3 %collective-permute-start.19 = (bf16[1024,512]{1,0:T(8,128)(2,1)}, bf16[1024,512]{1,0:T(8,128)(2,1)}, u32[]{:S(2)}, u32[]{:S(2)}) collective-permute-start(bf16[1024,512]{1,0:T(8,128)(2,1)} %copy-done.12), channel_id=1, source_target_pairs={{0,3},{1,0},{2,1},{3,2},{4,7},{5,4},{6,5},{7,6},{8,11},{9,8},{10,9... | collective-permute-start | bytes 3145736 | tf_op jit(solution)/shard_map/ppermute | solution.py:34
  121.7 18.9 %all-to-all-start.3 = ((bf16[4,2,256,256]{3,2,1,0:T(8,128)(2,1)}), bf16[4,2,256,256]{3,2,1,0:T(8,128)(2,1)}, u32[]{:S(2)}, u32[]{:S(2)}) async-start(bf16[4,2,256,256]{3,2,1,0:T(8,128)(2,1)} %select_blocks.5), calls=%async_computation.3 | async-start | bytes 2097152 | tf_op jit(solution)/shard_map/all_to_all | solution.py:52
  126.8 3.6 %collective-permute-start.17 = (bf16[1,256,256]{2,1,0:T(8,128)(2,1)S(1)}, bf16[1,256,256]{2,1,0:T(8,128)(2,1)S(1)}, u32[]{:S(2)}, u32[]{:S(2)}) collective-permute-start(bf16[1,256,256]{2,1,0:T(8,128)(2,1)S(1)} %broadcast_select_fusion.2), channel_id=1, source_target_pairs={{0,64},{4,68},{8,72},{12,76},{16,80},{20,84},{24,88},{28,92},{128,... | collective-permute-start | bytes 393224 | tf_op jit(solution)/shard_map/ppermute | solution.py:44
  130.4 21.0 %copy-start.1 = (f32[1024,128]{1,0:T(8,128)S(1)}, f32[1024,128]{1,0:T(8,128)}, u32[]{:S(2)}) copy-start(f32[1024,128]{1,0:T(8,128)} %get-tuple-element.94.sine) | copy-start | bytes 1572868
  140.6 10.8 %copy-start.10 = (bf16[1024,512]{1,0:T(8,128)(2,1)}, bf16[1024,512]{1,0:T(8,128)(2,1)S(1)}, u32[]{:S(2)}) copy-start(bf16[1024,512]{1,0:T(8,128)(2,1)S(1)} %collective-permute-done.18.b) | copy-start | bytes 3145732
  140.6 17.4 %all-to-all-start.4 = ((bf16[4,2,256,256]{3,2,1,0:T(8,128)(2,1)}), bf16[4,2,256,256]{3,2,1,0:T(8,128)(2,1)S(1)}, u32[]{:S(2)}, u32[]{:S(2)}) async-start(bf16[4,2,256,256]{3,2,1,0:T(8,128)(2,1)} %select_blocks.4), calls=%async_computation.4 | async-start | bytes 2097152 | tf_op jit(solution)/shard_map/all_to_all | solution.py:52
  145.3 12.0 %collective-permute-start.20 = (bf16[1,256,256]{2,1,0:T(8,128)(2,1)S(1)}, bf16[1,256,256]{2,1,0:T(8,128)(2,1)S(1)}, u32[]{:S(2)}, u32[]{:S(2)}) collective-permute-start(bf16[1,256,256]{2,1,0:T(8,128)(2,1)S(1)} %broadcast_select_fusion), channel_id=1, source_target_pairs={{0,32},{4,36},{8,40},{12,44},{16,48},{20,52},{24,56},{28,60},{64,9... | collective-permute-start | bytes 393224 | tf_op jit(solution)/shard_map/ppermute | solution.py:44
  146.6 14.7 %collective-permute-start.21 = (bf16[4,2,256,256]{3,2,1,0:T(8,128)(2,1)}, bf16[4,2,256,256]{3,2,1,0:T(8,128)(2,1)}, u32[]{:S(2)}, u32[]{:S(2)}) collective-permute-start(bf16[4,2,256,256]{3,2,1,0:T(8,128)(2,1)} %all-to-all-done.1.refs_0_), channel_id=1, source_target_pairs={{0,4},{4,0},{8,12},{12,8},{16,20},{20,16},{24,28},{28,24},{32,36},... | collective-permute-start | bytes 3145736 | tf_op jit(solution)/shard_map/ppermute | solution.py:57
  150.9 10.4 %collective-permute-start.22 = (bf16[4,2,256,256]{3,2,1,0:T(8,128)(2,1)}, bf16[4,2,256,256]{3,2,1,0:T(8,128)(2,1)}, u32[]{:S(2)}, u32[]{:S(2)}) collective-permute-start(bf16[4,2,256,256]{3,2,1,0:T(8,128)(2,1)} %all-to-all-done.2.refs_1_), channel_id=1, source_target_pairs={{0,4},{4,0},{8,12},{12,8},{16,20},{20,16},{24,28},{28,24},{32,36},... | collective-permute-start | bytes 3145736 | tf_op jit(solution)/shard_map/ppermute | solution.py:57
  151.0 10.4 %collective-permute-start.23 = (bf16[4,2,256,256]{3,2,1,0:T(8,128)(2,1)}, bf16[4,2,256,256]{3,2,1,0:T(8,128)(2,1)}, u32[]{:S(2)}, u32[]{:S(2)}) collective-permute-start(bf16[4,2,256,256]{3,2,1,0:T(8,128)(2,1)} %all-to-all-done.3.refs_2_), channel_id=1, source_target_pairs={{0,4},{4,0},{8,12},{12,8},{16,20},{20,16},{24,28},{28,24},{32,36},... | collective-permute-start | bytes 3145736 | tf_op jit(solution)/shard_map/ppermute | solution.py:57
  151.4 1.2 copy-start.7
  152.6 1.2 copy-start.9
  153.9 1.2 copy-start.11
  158.0 5.7 %collective-permute-start.24 = (bf16[4,2,256,256]{3,2,1,0:T(8,128)(2,1)S(1)}, bf16[4,2,256,256]{3,2,1,0:T(8,128)(2,1)S(1)}, u32[]{:S(2)}, u32[]{:S(2)}) collective-permute-start(bf16[4,2,256,256]{3,2,1,0:T(8,128)(2,1)S(1)} %all-to-all-done.4.refs_6_), channel_id=1, source_target_pairs={{0,4},{4,0},{8,12},{12,8},{16,20},{20,16},{24,28},{28,24},{32,36},... | collective-permute-start | bytes 3145736 | tf_op jit(solution)/shard_map/ppermute | solution.py:57
